TPU v7x, 32 devices: a whole 2x2x4 slice. The times are simulated.
32 devices in a mesh: ctx: 4 (over y, x), exp: 8 (over z, core).
Axes of the slice: x: 2, y: 2, z: 4, core: 2. Of those that a mesh axis runs over, the one named last changes fastest.
Arguments:
- queries: bfloat16 [8, 512, 2048], P('exp', 'ctx'), may hold values from -6 to 6
- key_rows: bfloat16 [8, 512, 256], P('exp', 'ctx'), may hold values from -6 to 6
- value_matrix: bfloat16 [8, 512, 256], P('exp', 'ctx'), may hold values from -4 to 4
- hidden: bfloat16 [8, 512, 2880], P('exp', 'ctx'), may hold values from -30 to 30
- out_weight: bfloat16 [2048, 2880], P('ctx'), may hold values from -0.125 to 0.125
- norm_gain: float32 [2880], replicated, may hold values from 0.1 to 1.9
- block_order: int32 [8], replicated, may hold values from 0 to 7, each once
- expert_ids: int32 [8, 512, 4], P('exp', 'ctx'), may hold values from 0 to 15, all different within a row; in each aligned block of 128 rows (0 to 127, 128 to 255, ..., all dimensions but the last counted through in order) at most 64 rows name the same one
- route_weights: float32 [8, 512, 4], P('exp', 'ctx'), may hold values from 0.1 to 0.6
- gate_up_weight: bfloat16 [32, 2880, 1440], P(('ctx', 'exp')), may hold values from -0.109375 to 0.109375
- down_weight: bfloat16 [32, 720, 2880], P(('ctx', 'exp')), may hold values from -0.15625 to 0.15625
Outputs:
- layer_out: bfloat16 [8, 512, 2880], P('exp', 'ctx')
Inputs may be any that keep to these rules, and one draw needn't show every extreme that they name: `expert_ids`: the 128 rows of one device (aligned blocks of rows) name any one expert at most 64 times, a bound that some block reaches.
All inputs are finite; a program needn't handle non-finite values.
Results may differ from a plain program's by a relative error of at most 0.017.
Values may be sent and summed in bfloat16 or wider, within the bound.
No kernel may reach another device: no remote copies, remote signals or barrier semaphores. Data moves between devices by JAX's collectives and lax.ppermute only.
A program may use at most 128 MiB of HBM per device.

v0:
```python
import functools

import jax
import jax.numpy as jnp
from jax import lax
from jax.experimental import pallas as pl
from jax.experimental.pallas import tpu as pltpu
from jax.sharding import PartitionSpec as P

D = 2880
QUERY_HEADS = 32
KEY_VALUE_HEADS = 4
HEAD_SIZE = 64
TOPK = 4


negative_large = -1e30


def ctx_swap(rows, distance):
    if distance == 0:
        return rows
    count = lax.axis_size("ctx")
    return lax.ppermute(rows, "ctx", [(i, i ^ distance) for i in range(count)])


def plane_shift(rows, planes):
    count = lax.axis_size("exp")
    if (2 * planes) % count == 0:
        return rows
    return lax.ppermute(rows, "exp", [(i, (i + 2 * planes) % count) for i in range(count)])


def core_swap(rows):
    count = lax.axis_size("exp")
    return lax.ppermute(rows, "exp", [(i, i ^ 1) for i in range(count)])

ANY_SPEC = pl.BlockSpec(memory_space=pl.ANY)
SMEM_SPEC = pl.BlockSpec(memory_space=pltpu.SMEM)
VMEM_SPEC = pl.BlockSpec(memory_space=pltpu.VMEM)
SMALL_COST = pl.CostEstimate(flops=1, bytes_accessed=1, transcendentals=0)


def nt_dot(left, right):
    return lax.dot_general(
        left, right, (((1,), (1,)), ((), ())), preferred_element_type=jnp.float32
    )


def nn_dot(left, right):
    return jnp.dot(left, right, preferred_element_type=jnp.float32)


def merged(block):
    return block.reshape(block.shape[0] * block.shape[1], block.shape[2])


def start_copies(pairs, sems, first=0):
    copies = [
        pltpu.make_async_copy(source, target, sems.at[first + i])
        for i, (source, target) in enumerate(pairs)
    ]
    for copy in copies:
        copy.start()
    return copies


def pack_kernel(ctx_count, ctx_ref, q_ref, k_ref, v_ref, *refs):
    out_refs, (q_buf, k_buf, v_buf, sems) = refs[:ctx_count], refs[ctx_count:]
    heads_here = QUERY_HEADS // ctx_count
    group = QUERY_HEADS // KEY_VALUE_HEADS
    width = heads_here * HEAD_SIZE
    rows = q_ref.shape[0]
    for copy in start_copies([(k_ref, k_buf), (v_ref, v_buf), (q_ref, q_buf)], sems):
        copy.wait()
    low = lax.broadcasted_iota(jnp.int32, (rows, 2 * HEAD_SIZE), 1) < HEAD_SIZE
    for d in range(ctx_count):
        to = ctx_ref[0] ^ d
        head = (to * heads_here) // group
        odd = (head % 2) == 1
        pair = pl.ds(pl.multiple_of((head // 2) * 2 * HEAD_SIZE, 2 * HEAD_SIZE), 2 * HEAD_SIZE)
        keys = k_buf[:, pair].astype(jnp.float32)
        values = v_buf[:, pair].astype(jnp.float32)
        keys = jnp.where(odd, pltpu.roll(keys, HEAD_SIZE, 1), keys)
        values = jnp.where(odd, values, pltpu.roll(values, HEAD_SIZE, 1))
        columns = pl.ds(pl.multiple_of(to * width, width), width)
        out_refs[d][:, :width] = q_buf[:, columns]
        out_refs[d][:, width:] = jnp.where(low, keys, values).astype(jnp.bfloat16)


def pack(ctx_scalar, queries, keys, values, ctx_count):
    rows, width = queries.shape[0], queries.shape[1] // ctx_count
    shape = jax.ShapeDtypeStruct((rows, width + 2 * HEAD_SIZE), jnp.bfloat16)
    return pl.pallas_call(
        functools.partial(pack_kernel, ctx_count),
        out_shape=[shape] * ctx_count,
        in_specs=[SMEM_SPEC] + [ANY_SPEC] * 3,
        out_specs=[VMEM_SPEC] * ctx_count,
        scratch_shapes=[pltpu.VMEM(x.shape, x.dtype) for x in (queries, keys, values)]
        + [pltpu.SemaphoreType.DMA((3,))],
        compiler_params=pltpu.CompilerParams(vmem_limit_bytes=56 << 20),
        cost_estimate=SMALL_COST,
    )(ctx_scalar, queries, keys, values)


def copy_kernel(source_ref, *refs):
    refs[-1][...] = source_ref[...]


def copy_after(source, after):
    return pl.pallas_call(
        copy_kernel,
        out_shape=jax.ShapeDtypeStruct(source.shape, source.dtype),
        in_specs=[VMEM_SPEC] + [ANY_SPEC] * len(after),
        out_specs=VMEM_SPEC,
        compiler_params=pltpu.CompilerParams(vmem_limit_bytes=20 << 20),
        cost_estimate=SMALL_COST,
    )(source, *after)


def attend_kernel(dests, ctx_count, ctx_ref, order_ref, weight_ref, *refs):
    out_refs, (weight_buf, got_refs, sems) = refs[-3 - len(dests) : -3], refs[-3:]
    hidden_ref = refs[ctx_count]
    copies = start_copies([(refs[d], got_refs.at[d]) for d in range(ctx_count)], sems)
    weight_copy = start_copies([(weight_ref, weight_buf)], sems, ctx_count)[0]
    for copy in copies:
        copy.wait()
    heads_here = QUERY_HEADS // ctx_count
    width = heads_here * HEAD_SIZE
    rows = got_refs.shape[1]
    block = rows // 2
    me = ctx_ref[0]
    lanes = lax.broadcasted_iota(jnp.int32, (rows, 2 * HEAD_SIZE), 1) < HEAD_SIZE
    keys, values, key_pos = [], [], []
    place = lax.broadcasted_iota(jnp.int32, (1, rows), 1)
    for d in range(ctx_count):
        both = got_refs[d, :, width:].astype(jnp.float32)
        other = pltpu.roll(both, HEAD_SIZE, 1)
        scaled = jnp.where(lanes, both, other) * HEAD_SIZE ** (-0.5)
        keys.append(scaled.astype(jnp.bfloat16))
        values.append(jnp.where(lanes, other, both).astype(jnp.bfloat16))
        slot = 2 * (me ^ d)
        first, second = order_ref[slot] * block, order_ref[slot + 1] * block - block
        key_pos.append(place + jnp.where(place < block, first, second))
    keys = jnp.concatenate(keys, axis=0)
    values = jnp.concatenate(values, axis=0)
    key_pos = jnp.concatenate(key_pos, axis=1)
    row = lax.broadcasted_iota(jnp.int32, (rows, 1), 0)
    stacked, visible, attended = [], [], []
    for d in dests:
        slot = 2 * (me ^ d)
        first, second = order_ref[slot] * block, order_ref[slot + 1] * block - block
        query_pos = row + jnp.where(row < block, first, second)
        visible += [key_pos <= query_pos] * heads_here
        for pair in range(heads_here // 2):
            both = got_refs[d, :, pair * 2 * HEAD_SIZE : (pair + 1) * 2 * HEAD_SIZE]
            for side in range(2):
                stacked.append(jnp.where(lanes == (side == 0), both, jnp.zeros_like(both)))
    scores = nt_dot(jnp.concatenate(stacked, axis=0), keys)
    scores = jnp.where(jnp.concatenate(visible, axis=0), scores, negative_large)
    probs = jnp.exp(scores - jnp.max(scores, axis=-1, keepdims=True))
    total = jnp.sum(probs, axis=-1, keepdims=True)
    mixed = nn_dot(probs.astype(jnp.bfloat16), values) / total
    mixed = [mixed[i * rows : (i + 1) * rows] for i in range(len(stacked))]
    for i in range(len(dests)):
        pairs = []
        for head in range(i * heads_here, (i + 1) * heads_here, 2):
            pairs.append(jnp.where(lanes, mixed[head], mixed[head + 1]).astype(jnp.bfloat16))
        attended.append(jnp.concatenate(pairs, axis=1))
    weight_copy.wait()
    parts = nt_dot(jnp.concatenate(attended, axis=0), weight_buf[...])
    for i, (out_ref, d) in enumerate(zip(out_refs, dests)):
        part = parts[i * rows : (i + 1) * rows]
        if d == 0:
            eye = lax.broadcasted_iota(jnp.int32, (rows, rows), 1) == row
            part = part + nt_dot(eye.astype(jnp.bfloat16), hidden_ref[...])
        out_ref[...] = part.astype(out_ref.dtype).reshape(out_ref.shape)


def attend(dests, ctx_scalar, order, weight, got, hidden, after):
    ctx_count = len(got)
    rows, columns = got[0].shape[0], weight.shape[0]
    shapes = [
        jax.ShapeDtypeStruct((2, rows // 2, columns), jnp.bfloat16 if d else jnp.float32)
        for d in dests
    ]
    extra = [hidden] if 0 in dests else []
    work = len(dests) * rows * weight.shape[1]
    return pl.pallas_call(
        functools.partial(attend_kernel, dests, ctx_count),
        out_shape=shapes,
        in_specs=[SMEM_SPEC, SMEM_SPEC]
        + [ANY_SPEC] * (1 + ctx_count)
        + [VMEM_SPEC] * len(extra)
        + [ANY_SPEC] * len(after),
        out_specs=[VMEM_SPEC] * len(dests),
        scratch_shapes=[
            pltpu.VMEM(weight.shape, weight.dtype),
            pltpu.VMEM((ctx_count,) + got[0].shape, got[0].dtype),
            pltpu.SemaphoreType.DMA((ctx_count + 1,)),
        ],
        compiler_params=pltpu.CompilerParams(vmem_limit_bytes=56 << 20),
        cost_estimate=SMALL_COST,
    )(ctx_scalar, order, weight, *got, *extra, *after)


def pick_and_mix(ctx_count, capacity, ctx_ref, plane_ref, held, route, out_refs, mix_ref):
    tokens = held.shape[0]
    count = ctx_count * capacity
    lane = lax.broadcasted_iota(jnp.int32, (1, count), 1)
    partner = ctx_ref[0] ^ (lane // capacity)
    wanted = (partner * plane_ref[1] + plane_ref[0]).astype(jnp.float32)
    member = jnp.zeros((tokens, count), jnp.float32)
    weight = jnp.zeros((tokens, count), jnp.float32)
    for k in range(TOPK):
        chosen = route[:, k : k + 1] == wanted
        member = jnp.where(chosen, 1.0, member)
        weight = jnp.where(chosen, route[:, TOPK + k : TOPK + k + 1], weight)
    row = lax.broadcasted_iota(jnp.int32, (tokens, tokens), 0)
    earlier = lax.broadcasted_iota(jnp.int32, (tokens, tokens), 1) < row
    rank = nn_dot(earlier.astype(jnp.bfloat16), member.astype(jnp.bfloat16))
    slot = (lane % capacity).astype(jnp.float32)
    placed = jnp.where(rank == slot, member, 0.0)
    mix_ref[...] = (placed * weight).astype(jnp.bfloat16)
    picked = nn_dot(placed.T.astype(jnp.bfloat16), held).astype(jnp.bfloat16)
    for d, out_ref in enumerate(out_refs):
        out_ref[...] = picked[d * capacity : (d + 1) * capacity]


def norm_kernel(part_count, ctx_ref, plane_ref, gain_ref, route_ref, *refs):
    part_refs = refs[:part_count]
    residual_ref, normed_ref, mix_ref, *out_refs = refs[-3 - part_count :]
    capacity, columns = out_refs[0].shape
    total = merged(part_refs[0][...])
    for part_ref in part_refs[1:]:
        total = total + merged(part_ref[...]).astype(jnp.float32)
    residual = total.astype(jnp.bfloat16)
    residual_ref[...] = residual.reshape(residual_ref.shape)
    res_float = residual.astype(jnp.float32)
    mean = jnp.mean(res_float * res_float, axis=-1, keepdims=True)
    normed = (res_float * lax.rsqrt(mean + 1e-05) * gain_ref[...]).astype(jnp.bfloat16)
    route = route_ref[...]
    normed_ref[:, :, :columns] = normed.reshape(residual_ref.shape)
    normed_ref[:, :, columns:] = route.reshape(normed_ref.shape[:2] + route.shape[1:])
    pick_and_mix(
        part_count,
        capacity,
        ctx_ref,
        plane_ref,
        normed,
        route.astype(jnp.float32),
        out_refs,
        mix_ref,
    )


def pick_shapes(ctx_count, capacity, tokens, columns):
    slot = jax.ShapeDtypeStruct((capacity, columns), jnp.bfloat16)
    return [jax.ShapeDtypeStruct((tokens, ctx_count * capacity), jnp.bfloat16)] + [slot] * ctx_count


def norm_and_pick(ctx_scalar, plane_scalars, gain, route, parts, capacity, after):
    _, half, columns = parts[0].shape
    tokens, extra = route.shape
    return pl.pallas_call(
        functools.partial(norm_kernel, len(parts)),
        out_shape=[
            jax.ShapeDtypeStruct((2, half, columns), jnp.bfloat16),
            jax.ShapeDtypeStruct((2, half, columns + extra), jnp.bfloat16),
        ]
        + pick_shapes(len(parts), capacity, tokens, columns),
        in_specs=[SMEM_SPEC] * 2 + [VMEM_SPEC] * (2 + len(parts)) + [ANY_SPEC] * len(after),
        out_specs=[VMEM_SPEC] * (3 + len(parts)),
        compiler_params=pltpu.CompilerParams(vmem_limit_bytes=12 << 20),
        cost_estimate=SMALL_COST,
    )(ctx_scalar, plane_scalars, gain, route, *parts, *after)


def pick_kernel(ctx_count, ctx_ref, plane_ref, held_ref, *refs):
    mix_ref, *out_refs = refs[-1 - ctx_count :]
    capacity, columns = out_refs[0].shape
    held = merged(held_ref[:, :, :columns])
    route = merged(held_ref[:, :, columns:]).astype(jnp.float32)
    pick_and_mix(ctx_count, capacity, ctx_ref, plane_ref, held, route, out_refs, mix_ref)


def pick_rows(ctx_scalar, plane_scalars, held, like, after):
    ctx_count = len(like)
    capacity, columns = like[0].shape
    return pl.pallas_call(
        functools.partial(pick_kernel, ctx_count),
        out_shape=pick_shapes(ctx_count, capacity, 2 * held.shape[1], columns),
        in_specs=[SMEM_SPEC] * 2 + [VMEM_SPEC] + [ANY_SPEC] * len(after),
        out_specs=[VMEM_SPEC] * (1 + ctx_count),
        compiler_params=pltpu.CompilerParams(vmem_limit_bytes=6 << 20),
        cost_estimate=SMALL_COST,
    )(ctx_scalar, plane_scalars, held, *after)


def expert_kernel(ctx_count, tile, *refs):
    row_refs, refs = refs[:ctx_count], refs[ctx_count:]
    gate_up_refs, down_refs = refs[:2], refs[2:4]
    out_refs, total_ref = refs[-ctx_count - 1 : -1], refs[-1]
    capacity = row_refs[0].shape[0]

    def add_tile(i, carry):
        routed = jnp.concatenate([row_ref[...] for row_ref in row_refs], axis=0)
        here = pl.ds(pl.multiple_of(i * tile, tile), tile)
        added = None
        for gate_up_ref, down_ref in zip(gate_up_refs, down_refs):
            gate = nt_dot(routed, gate_up_ref[0, here])
            up = nt_dot(routed, gate_up_ref[1, here])
            activated = gate * jax.nn.sigmoid(1.702 * gate) * (up + 1.0)
            term = nn_dot(activated.astype(jnp.bfloat16), down_ref[here])
            added = term if added is None else added + term

        @pl.when(i == 0)
        def _():
            total_ref[...] = added

        @pl.when(i > 0)
        def _():
            total_ref[...] += added

        return carry

    lax.fori_loop(0, down_refs[0].shape[0] // tile, add_tile, 0)
    for d, out_ref in enumerate(out_refs):
        out_ref[...] = total_ref[d * capacity : (d + 1) * capacity].astype(jnp.bfloat16)


def expert(rows, gate_ups, downs, after):
    ctx_count = len(rows)
    capacity, columns = rows[0].shape
    tile = downs[0].shape[0] // 3
    return pl.pallas_call(
        functools.partial(expert_kernel, ctx_count, tile),
        out_shape=[jax.ShapeDtypeStruct((capacity, columns), jnp.bfloat16)] * ctx_count,
        in_specs=[VMEM_SPEC] * (ctx_count + 4) + [ANY_SPEC] * len(after),
        out_specs=[VMEM_SPEC] * ctx_count,
        scratch_shapes=[pltpu.VMEM((ctx_count * capacity, columns), jnp.float32)],
        compiler_params=pltpu.CompilerParams(vmem_limit_bytes=16 << 20),
        cost_estimate=SMALL_COST,
    )(*rows, *gate_ups, *downs, *after)


def mix_kernel(ctx_count, extra_count, mix_ref, *refs):
    back_refs, extra_refs = refs[:ctx_count], refs[ctx_count : ctx_count + extra_count]
    out_ref = refs[-1]
    back = jnp.concatenate([back_ref[...] for back_ref in back_refs], axis=0)
    total = nn_dot(mix_ref[...], back)
    for extra_ref in extra_refs:
        total = total + merged(extra_ref[...]).astype(jnp.float32)
    out_ref[...] = total.astype(out_ref.dtype).reshape(out_ref.shape)


def mix_rows(mix, back, extra, after, dtype=jnp.bfloat16):
    tokens, count = mix.shape
    columns = back[0].shape[1]
    shape = (2, tokens // 2, columns)
    return pl.pallas_call(
        functools.partial(mix_kernel, len(back), len(extra)),
        out_shape=jax.ShapeDtypeStruct(shape, dtype),
        in_specs=[VMEM_SPEC] * (1 + len(back) + len(extra)) + [ANY_SPEC] * len(after),
        out_specs=VMEM_SPEC,
        compiler_params=pltpu.CompilerParams(vmem_limit_bytes=8 << 20),
        cost_estimate=SMALL_COST,
    )(mix, *back, *extra, *after)


def sum_kernel(part_count, *refs):
    total = refs[0][...]
    for part_ref in refs[1:part_count]:
        total = total + part_ref[...].astype(jnp.float32)
    refs[-1][...] = total.astype(jnp.bfloat16)


def sum_parts(parts, after):
    return pl.pallas_call(
        functools.partial(sum_kernel, len(parts)),
        out_shape=jax.ShapeDtypeStruct(parts[0].shape, jnp.bfloat16),
        in_specs=[VMEM_SPEC] * len(parts) + [ANY_SPEC] * len(after),
        out_specs=VMEM_SPEC,
        compiler_params=pltpu.CompilerParams(vmem_limit_bytes=4 << 20),
        cost_estimate=SMALL_COST,
    )(*parts, *after)


def local(
    queries,
    key_rows,
    value_matrix,
    hidden,
    out_weight,
    norm_gain,
    block_order,
    expert_ids,
    route_weights,
    gate_up_weight,
    down_weight,
):
    ctx_count = lax.axis_size("ctx")
    planes = lax.axis_size("exp") // 2
    ctx_scalar = lax.axis_index("ctx").astype(jnp.int32).reshape(1)
    plane_index = (lax.axis_index("exp") // 2).astype(jnp.int32)
    plane_scalars = jnp.stack([plane_index, jnp.full_like(plane_index, planes)])
    token_count = queries.shape[1]
    experts = ctx_count * planes
    capacity = 2 * token_count * TOPK // experts
    last = ctx_count - 1

    packed = pack(ctx_scalar, queries[0], key_rows[0], value_matrix[0], ctx_count)
    got = [ctx_swap(packed[d], d) for d in range(ctx_count)]

    gate_up_mine = jnp.swapaxes(gate_up_weight[0], 0, 1)
    down_mine = down_weight[0]
    half = down_mine.shape[0]
    got, gate_up_mine, down_mine = lax.optimization_barrier((got, gate_up_mine, down_mine))

    weight = jnp.swapaxes(out_weight, 0, 1)
    partners = tuple(range(last, 0, -1))
    parts = list(attend(partners, ctx_scalar, block_order, weight, got, None, []))
    swapped = [core_swap(gate_up_mine), core_swap(down_mine)]
    hidden_columns = jnp.swapaxes(hidden[0], 0, 1)
    own = attend((0,), ctx_scalar, block_order, weight, got, hidden_columns, parts[:1])
    parts = [ctx_swap(part, last - i) for i, part in enumerate(parts)]
    other = [copy_after(w, list(own)) for w in swapped]
    gate_ups = [w.reshape(2, half, D) for w in (gate_up_mine, other[0])]
    downs = [down_mine, other[1]]

    route = jnp.concatenate(
        [expert_ids[0].astype(jnp.bfloat16), route_weights[0].astype(jnp.bfloat16)], axis=1
    )
    route = jnp.pad(route, ((0, 0), (0, -D % 128 - 2 * TOPK)))
    residual, held, mix, *rows = norm_and_pick(
        ctx_scalar, plane_scalars, norm_gain[None], route, list(own) + parts, capacity, other
    )

    def spread(blocks):
        return [ctx_swap(blocks[d], d) for d in range(ctx_count)]

    mixes = [mix]
    arrived = [spread(rows)]
    back = [None] * planes

    def run_expert(s, after):
        result = expert(arrived[s], gate_ups, downs, after)
        if s > 0:
            back[s] = spread(result)
        return list(result)

    def run_mix(s, carried, after):
        part = mix_rows(mixes[s], back[s], carried, after)
        return [part], [plane_shift(part, 1)]

    done, carried = [], []
    for s in range(1, planes):
        held = plane_shift(held, 1)
        mix, *rows = pick_rows(ctx_scalar, plane_scalars, held, rows, arrived[s - 1][1:] + done[:1])
        held, rows = lax.optimization_barrier((held, rows))
        mixes.append(mix)
        arrived.append(spread(rows))
        done = run_expert(s - 1, list(rows[:1]))
        if s == 1:
            own_result = done
        if s > 2:
            done, carried = run_mix(s - 2, carried, done)
    done = run_expert(planes - 1, done)
    own_result, _ = lax.optimization_barrier((own_result, done))
    back[0] = spread(own_result)
    for s in range(max(planes - 2, 1), planes):
        done, carried = run_mix(s, carried, done)
    own = mix_rows(mixes[0], back[0], [residual], done, jnp.float32)
    out = sum_parts([own] + carried, [])
    return out.reshape(1, token_count, D)


def solution(mesh):
    return jax.shard_map(
        local,
        mesh=mesh,
        in_specs=(
            P("exp", "ctx", None),
            P("exp", "ctx", None),
            P("exp", "ctx", None),
            P("exp", "ctx", None),
            P("ctx", None),
            P(),
            P(),
            P("exp", "ctx", None),
            P("exp", "ctx", None),
            P(("ctx", "exp"), None, None),
            P(("ctx", "exp"), None, None),
        ),
        out_specs=P("exp", "ctx", None),
        check_vma=False,
    )
```

profile of v0, /device:TPU:0, one launch (start us, length us, event | category | flops | bytes accessed | tf_op | source)
XLA Modules:
  0.0 209.0 jit_solution(2595782814869331750)
XLA Ops:
  0.0 2.1 %shard_map.109 = (bf16[128,640]{1,0:T(8,128)(2,1)}, bf16[128,640]{1,0:T(8,128)(2,1)}, bf16[128,640]{1,0:T(8,128)(2,1)}, bf16[128,640]{1,0:T(8,128)(2,1)}) custom-call(s32[1]{0:T(128)} %bitcast.ctx_ref, bf16[128,2048]{1,0:T(8,128)(2,1)} %bitcast.42, bf16[128,256]{1,0:T(8,128)(2,1)} %bitcast.43, bf16[128,256]{1,0:T(8,128)(2,1)} %bitcast.44), custom_call_target="tpu_custom_call" | custom-call | flops 1 | bytes 1 | tf_op jit(solution)/shard_map/pallas_call | solution.py:94
  2.1 3.0 %collective-permute-start = (bf16[128,640]{1,0:T(8,128)(2,1)}, bf16[128,640]{1,0:T(8,128)(2,1)S(1)}, u32[]{:S(2)}, u32[]{:S(2)}) collective-permute-start(bf16[128,640]{1,0:T(8,128)(2,1)} %get-tuple-element.75), channel_id=1, source_target_pairs={{0,8},{8,0},{16,24},{24,16},{1,9},{9,1},{17,25},{25,17},{2,10},{10... | collective-permute-start | bytes 491528 | tf_op jit(solution)/shard_map/ppermute | solution.py:24
  5.1 1.5 collective-permute-start.1
  6.7 3.7 %collective-permute-done.refs_1_ = bf16[128,640]{1,0:T(8,128)(2,1)S(1)} collective-permute-done((bf16[128,640]{1,0:T(8,128)(2,1)}, bf16[128,640]{1,0:T(8,128)(2,1)S(1)}, u32[]{:S(2)}, u32[]{:S(2)}) %collective-permute-start) | collective-permute-done | bytes 163872 | tf_op jit(solution)/shard_map/ppermute | solution.py:24
  10.4 4.1 %collective-permute-done.1.refs_2_ = bf16[128,640]{1,0:T(8,128)(2,1)S(1)} collective-permute-done((bf16[128,640]{1,0:T(8,128)(2,1)}, bf16[128,640]{1,0:T(8,128)(2,1)S(1)}, u32[]{:S(2)}, u32[]{:S(2)}) %collective-permute-start.1) | collective-permute-done | bytes 163872 | tf_op jit(solution)/shard_map/ppermute | solution.py:24
  15.2 8.7 %shard_map.110 = (bf16[2,64,2880]{2,1,0:T(8,128)(2,1)}, bf16[2,64,2880]{2,1,0:T(8,128)(2,1)}, bf16[2,64,2880]{2,1,0:T(8,128)(2,1)}) custom-call(s32[1]{0:T(128)} %bitcast.ctx_ref, s32[8]{0:T(128)} %order_ref.3, bf16[2880,512]{1,0:T(8,128)(2,1)} %bitcast.39, bf16[128,640]{1,0:T(8,128)(2,1)} %get-tuple-element.78.refs_0_, bf16[128,640]{1,0:T(8,128)(2,1)} %copy-done.2, ...), custom_call_target="tpu_custom_call" | custom-call | flops 1 | bytes 1 | tf_op jit(solution)/shard_map/pallas_call | solution.py:189
  23.9 1.6 collective-permute-start.3
  25.5 1.1 collective-permute-start.4
  26.6 0.9 collective-permute-start.5
  27.8 6.6 %shard_map.111.refs_0_ = f32[2,64,2880]{2,1,0:T(8,128)} custom-call(s32[1]{0:T(128)} %bitcast.ctx_ref, s32[8]{0:T(128)} %order_ref.3, bf16[2880,512]{1,0:T(8,128)(2,1)} %bitcast.40, bf16[128,640]{1,0:T(8,128)(2,1)} %get-tuple-element.78.refs_0_, bf16[128,640]{1,0:T(8,128)(2,1)} %copy-done.2, bf16[128,640]{1,0:T(8,128)(2,1)} %copy-done.3, ...), custom_call_target="tpu_custom_call" | custom-call | flops 1 | bytes 1 | tf_op jit(solution)/shard_map/pallas_call | solution.py:189
  34.4 1.4 copy-done
  35.8 2.6 %shard_map.113.refs_5_.refs_7_ = bf16[720,2880]{1,0:T(8,128)(2,1)S(1)} custom-call(bf16[720,2880]{1,0:T(8,128)(2,1)} %collective-permute-done.7.source_ref, f32[2,64,2880]{2,1,0:T(8,128)S(1)} %copy-done), custom_call_target="tpu_custom_call" | custom-call | flops 1 | bytes 1 | tf_op jit(solution)/shard_map/pallas_call | solution.py:111
  38.5 4.3 %shard_map.112.refs_4_ = bf16[1440,2880]{1,0:T(8,128)(2,1)S(1)} custom-call(bf16[1440,2880]{1,0:T(8,128)(2,1)} %collective-permute-done.6.source_ref, f32[2,64,2880]{2,1,0:T(8,128)S(1)} %copy-done.1), custom_call_target="tpu_custom_call" | custom-call | flops 1 | bytes 1 | tf_op jit(solution)/shard_map/pallas_call | solution.py:111
  42.8 2.1 collective-permute-done.3.refs_1_
  44.9 15.1 %collective-permute-done.4.refs_2_ = bf16[2,64,2880]{2,1,0:T(8,128)(2,1)S(1)} collective-permute-done((bf16[2,64,2880]{2,1,0:T(8,128)(2,1)}, bf16[2,64,2880]{2,1,0:T(8,128)(2,1)S(1)}, u32[]{:S(2)}, u32[]{:S(2)}) %collective-permute-start.4) | collective-permute-done | bytes 737312 | tf_op jit(solution)/shard_map/ppermute | solution.py:24
  60.0 1.8 shard_map.114
  61.9 1.6 collective-permute-start.11
  63.5 1.0 collective-permute-start.8
  64.5 1.0 collective-permute-start.9
  65.5 1.5 collective-permute-start.10
  67.0 8.2 %collective-permute-done.8.refs_0_.refs_1_ = bf16[64,2880]{1,0:T(8,128)(2,1)S(1)} collective-permute-done((bf16[64,2880]{1,0:T(8,128)(2,1)S(1)}, bf16[64,2880]{1,0:T(8,128)(2,1)S(1)}, u32[]{:S(2)}, u32[]{:S(2)}) %collective-permute-start.8) | collective-permute-done | bytes 368672 | tf_op jit(solution)/shard_map/ppermute | solution.py:24
  75.2 7.5 %collective-permute-done.9.refs_1_.refs_2_ = bf16[64,2880]{1,0:T(8,128)(2,1)S(1)} collective-permute-done((bf16[64,2880]{1,0:T(8,128)(2,1)S(1)}, bf16[64,2880]{1,0:T(8,128)(2,1)S(1)}, u32[]{:S(2)}, u32[]{:S(2)}) %collective-permute-start.9) | collective-permute-done | bytes 368672 | tf_op jit(solution)/shard_map/ppermute | solution.py:24
  82.7 1.4 shard_map.115
  84.2 1.8 collective-permute-start.12
  86.0 0.9 collective-permute-start.13
  86.9 1.3 collective-permute-start.14
  88.1 1.3 collective-permute-start.15
  89.5 9.1 %shard_map.116 = (bf16[64,2880]{1,0:T(8,128)(2,1)S(1)}, bf16[64,2880]{1,0:T(8,128)(2,1)S(1)}, bf16[64,2880]{1,0:T(8,128)(2,1)S(1)}, bf16[64,2880]{1,0:T(8,128)(2,1)S(1)}) custom-call(bf16[64,2880]{1,0:T(8,128)(2,1)S(1)} %get-tuple-element.88.refs_0_, bf16[64,2880]{1,0:T(8,128)(2,1)S(1)} %collective-permute-done.8.refs_0_.refs_1_, ...), custom_call_target="tpu_custom_call" | custom-call | flops 1 | bytes 1 | tf_op jit(solution)/shard_map/pallas_call | solution.py:336
  98.6 5.1 %collective-permute-done.14.refs_1_.refs_2_ = bf16[64,2880]{1,0:T(8,128)(2,1)S(1)} collective-permute-done((bf16[64,2880]{1,0:T(8,128)(2,1)S(1)}, bf16[64,2880]{1,0:T(8,128)(2,1)S(1)}, u32[]{:S(2)}, u32[]{:S(2)}) %collective-permute-start.14) | collective-permute-done | bytes 368672 | tf_op jit(solution)/shard_map/ppermute | solution.py:24
  103.8 1.4 shard_map.117
  105.2 1.6 collective-permute-start.16
  106.8 1.1 collective-permute-start.17
  107.8 0.8 collective-permute-start.18
  108.7 1.6 collective-permute-start.19
  110.3 9.1 %shard_map.118 = (bf16[64,2880]{1,0:T(8,128)(2,1)S(1)}, bf16[64,2880]{1,0:T(8,128)(2,1)S(1)}, bf16[64,2880]{1,0:T(8,128)(2,1)S(1)}, bf16[64,2880]{1,0:T(8,128)(2,1)S(1)}) custom-call(bf16[64,2880]{1,0:T(8,128)(2,1)S(1)} %get-tuple-element.97.refs_8_.refs_0_, bf16[64,2880]{1,0:T(8,128)(2,1)S(1)} %collective-permute-done.13.refs_0_.refs_1_, ...), custom_call_target="tpu_custom_call" | custom-call | flops 1 | bytes 1 | tf_op jit(solution)/shard_map/pallas_call | solution.py:336
  119.4 1.1 collective-permute-start.23
  120.5 0.8 collective-permute-start.24
  121.3 1.6 collective-permute-start.25
  122.9 4.2 %collective-permute-done.19.refs_2_.refs_3_ = bf16[64,2880]{1,0:T(8,128)(2,1)S(1)} collective-permute-done((bf16[64,2880]{1,0:T(8,128)(2,1)S(1)}, bf16[64,2880]{1,0:T(8,128)(2,1)S(1)}, u32[]{:S(2)}, u32[]{:S(2)}) %collective-permute-start.19) | collective-permute-done | bytes 368672 | tf_op jit(solution)/shard_map/ppermute | solution.py:24
  127.1 1.4 shard_map.119
  128.5 0.9 collective-permute-start.20
  129.4 1.2 collective-permute-start.21
  130.6 9.1 %shard_map.120 = (bf16[64,2880]{1,0:T(8,128)(2,1)S(1)}, bf16[64,2880]{1,0:T(8,128)(2,1)S(1)}, bf16[64,2880]{1,0:T(8,128)(2,1)S(1)}, bf16[64,2880]{1,0:T(8,128)(2,1)S(1)}) custom-call(bf16[64,2880]{1,0:T(8,128)(2,1)S(1)} %get-tuple-element.114.refs_8_.refs_0_, bf16[64,2880]{1,0:T(8,128)(2,1)S(1)} %collective-permute-done.17.refs_0_.refs_1_, ...), custom_call_target="tpu_custom_call" | custom-call | flops 1 | bytes 1 | tf_op jit(solution)/shard_map/pallas_call | solution.py:336
  140.3 2.9 %collective-permute-done.25.refs_3_ = bf16[64,2880]{1,0:T(8,128)(2,1)S(1)} collective-permute-done((bf16[64,2880]{1,0:T(8,128)(2,1)S(1)}, bf16[64,2880]{1,0:T(8,128)(2,1)S(1)}, u32[]{:S(2)}, u32[]{:S(2)}) %collective-permute-start.25) | collective-permute-done | bytes 368672 | tf_op jit(solution)/shard_map/ppermute | solution.py:24
  143.6 0.8 collective-permute-start.35
  144.4 0.8 collective-permute-start.32
  145.2 1.6 collective-permute-start.22
  146.8 3.8 %collective-permute-done.20.refs_1_ = bf16[64,2880]{1,0:T(8,128)(2,1)S(1)} collective-permute-done((bf16[64,2880]{1,0:T(8,128)(2,1)S(1)}, bf16[64,2880]{1,0:T(8,128)(2,1)S(1)}, u32[]{:S(2)}, u32[]{:S(2)}) %collective-permute-start.20) | collective-permute-done | bytes 368672 | tf_op jit(solution)/shard_map/ppermute | solution.py:24
  150.6 1.2 collective-permute-start.33
  151.9 1.5 collective-permute-start.34
  153.3 14.1 %collective-permute-done.22.refs_3_ = bf16[64,2880]{1,0:T(8,128)(2,1)S(1)} collective-permute-done((bf16[64,2880]{1,0:T(8,128)(2,1)S(1)}, bf16[64,2880]{1,0:T(8,128)(2,1)S(1)}, u32[]{:S(2)}, u32[]{:S(2)}) %collective-permute-start.22) | collective-permute-done | bytes 368672 | tf_op jit(solution)/shard_map/ppermute | solution.py:24
  167.4 9.1 %shard_map.122 = (bf16[64,2880]{1,0:T(8,128)(2,1)S(1)}, bf16[64,2880]{1,0:T(8,128)(2,1)S(1)}, bf16[64,2880]{1,0:T(8,128)(2,1)S(1)}, bf16[64,2880]{1,0:T(8,128)(2,1)S(1)}) custom-call(bf16[64,2880]{1,0:T(8,128)(2,1)S(1)} %get-tuple-element.120.refs_8_.refs_0_, bf16[64,2880]{1,0:T(8,128)(2,1)S(1)} %collective-permute-done.20.refs_1_, ...), custom_call_target="tpu_custom_call" | custom-call | flops 1 | bytes 1 | tf_op jit(solution)/shard_map/pallas_call | solution.py:336
  177.6 0.8 collective-permute-start.29
  178.4 1.1 collective-permute-start.30
  179.6 1.5 collective-permute-start.31
  181.1 4.1 %collective-permute-done.29.refs_1_ = bf16[64,2880]{1,0:T(8,128)(2,1)S(1)} collective-permute-done((bf16[64,2880]{1,0:T(8,128)(2,1)S(1)}, bf16[64,2880]{1,0:T(8,128)(2,1)S(1)}, u32[]{:S(2)}, u32[]{:S(2)}) %collective-permute-start.29) | collective-permute-done | bytes 368672 | tf_op jit(solution)/shard_map/ppermute | solution.py:24
  185.2 3.2 %collective-permute-done.30.refs_2_ = bf16[64,2880]{1,0:T(8,128)(2,1)S(1)} collective-permute-done((bf16[64,2880]{1,0:T(8,128)(2,1)S(1)}, bf16[64,2880]{1,0:T(8,128)(2,1)S(1)}, u32[]{:S(2)}, u32[]{:S(2)}) %collective-permute-start.30) | collective-permute-done | bytes 368672 | tf_op jit(solution)/shard_map/ppermute | solution.py:24
  188.4 4.3 %collective-permute-done.31.refs_3_ = bf16[64,2880]{1,0:T(8,128)(2,1)S(1)} collective-permute-done((bf16[64,2880]{1,0:T(8,128)(2,1)S(1)}, bf16[64,2880]{1,0:T(8,128)(2,1)S(1)}, u32[]{:S(2)}, u32[]{:S(2)}) %collective-permute-start.31) | collective-permute-done | bytes 368672 | tf_op jit(solution)/shard_map/ppermute | solution.py:24
  192.7 1.1 collective-permute-done.36.refs_4_
  194.4 1.3 collective-permute-start.26
  196.4 1.4 collective-permute-start.28
  197.9 4.1 %collective-permute-done.26.refs_1_ = bf16[64,2880]{1,0:T(8,128)(2,1)S(1)} collective-permute-done((bf16[64,2880]{1,0:T(8,128)(2,1)S(1)}, bf16[64,2880]{1,0:T(8,128)(2,1)S(1)}, u32[]{:S(2)}, u32[]{:S(2)}) %collective-permute-start.26) | collective-permute-done | bytes 368672 | tf_op jit(solution)/shard_map/ppermute | solution.py:24
  202.0 5.3 %collective-permute-done.27.refs_2_ = bf16[64,2880]{1,0:T(8,128)(2,1)S(1)} collective-permute-done((bf16[64,2880]{1,0:T(8,128)(2,1)S(1)}, bf16[64,2880]{1,0:T(8,128)(2,1)S(1)}, u32[]{:S(2)}, u32[]{:S(2)}) %collective-permute-start.27) | collective-permute-done | bytes 368672 | tf_op jit(solution)/shard_map/ppermute | solution.py:24
  207.9 1.1 copy.16
  (66 shorter events, 5.2 us)
Async XLA Ops:
  0.0 27.5 %copy-start.5 = (f32[2880]{0:T(1024)S(1)}, f32[2880]{0:T(1024)}, u32[]{:S(2)}) copy-start(f32[2880]{0:T(1024)} %param.16) | copy-start | bytes 34564
  0.0 27.5 %copy-start.6 = (f32[1,128,4]{1,2,0:T(4,128)S(1)}, f32[1,128,4]{1,2,0:T(4,128)}, u32[]{:S(2)}) copy-start(f32[1,128,4]{1,2,0:T(4,128)} %param.19) | copy-start | bytes 6148
  0.0 27.5 %copy-start.7 = (s32[1,128,4]{1,2,0:T(4,128)S(1)}, s32[1,128,4]{1,2,0:T(4,128)}, u32[]{:S(2)}) copy-start(s32[1,128,4]{1,2,0:T(4,128)} %param.18) | copy-start | bytes 6148
  2.1 8.2 %collective-permute-start = (bf16[128,640]{1,0:T(8,128)(2,1)}, bf16[128,640]{1,0:T(8,128)(2,1)S(1)}, u32[]{:S(2)}, u32[]{:S(2)}) collective-permute-start(bf16[128,640]{1,0:T(8,128)(2,1)} %get-tuple-element.75), channel_id=1, source_target_pairs={{0,8},{8,0},{16,24},{24,16},{1,9},{9,1},{17,25},{25,17},{2,10},{10... | collective-permute-start | bytes 491528 | tf_op jit(solution)/shard_map/ppermute | solution.py:24
  5.1 9.4 %collective-permute-start.1 = (bf16[128,640]{1,0:T(8,128)(2,1)}, bf16[128,640]{1,0:T(8,128)(2,1)S(1)}, u32[]{:S(2)}, u32[]{:S(2)}) collective-permute-start(bf16[128,640]{1,0:T(8,128)(2,1)} %get-tuple-element.76), channel_id=1, source_target_pairs={{0,16},{8,24},{16,0},{24,8},{1,17},{9,25},{17,1},{25,9},{2,18},{10... | collective-permute-start | bytes 491528 | tf_op jit(solution)/shard_map/ppermute | solution.py:24
  6.6 7.9 %collective-permute-start.2 = (bf16[128,640]{1,0:T(8,128)(2,1)}, bf16[128,640]{1,0:T(8,128)(2,1)S(1)}, u32[]{:S(2)}, u32[]{:S(2)}) collective-permute-start(bf16[128,640]{1,0:T(8,128)(2,1)} %get-tuple-element.77), channel_id=1, source_target_pairs={{0,24},{8,16},{16,8},{24,0},{1,25},{9,17},{17,9},{25,1},{2,26},{10... | collective-permute-start | bytes 491528 | tf_op jit(solution)/shard_map/ppermute | solution.py:24
  10.4 4.7 %copy-start.2 = (bf16[128,640]{1,0:T(8,128)(2,1)}, bf16[128,640]{1,0:T(8,128)(2,1)S(1)}, u32[]{:S(2)}) copy-start(bf16[128,640]{1,0:T(8,128)(2,1)S(1)} %collective-permute-done.refs_1_) | copy-start | bytes 491524
  14.5 0.7 copy-start.3
  14.5 0.7 copy-start.4
  14.5 23.9 %collective-permute-start.6 = (bf16[1440,2880]{1,0:T(8,128)(2,1)}, bf16[1440,2880]{1,0:T(8,128)(2,1)}, u32[]{:S(2)}, u32[]{:S(2)}) collective-permute-start(bf16[1440,2880]{1,0:T(8,128)(2,1)} %bitcast.24), channel_id=1, source_target_pairs={{0,1},{1,0},{2,3},{3,2},{4,5},{5,4},{6,7},{7,6},{8,9},{9,8},{10,11... | collective-permute-start | bytes 24883208 | tf_op jit(solution)/shard_map/ppermute | solution.py:36
  14.6 19.8 %collective-permute-start.7 = (bf16[720,2880]{1,0:T(8,128)(2,1)}, bf16[720,2880]{1,0:T(8,128)(2,1)}, u32[]{:S(2)}, u32[]{:S(2)}) collective-permute-start(bf16[720,2880]{1,0:T(8,128)(2,1)} %bitcast.31), channel_id=1, source_target_pairs={{0,1},{1,0},{2,3},{3,2},{4,5},{5,4},{6,7},{7,6},{8,9},{9,8},{10,11... | collective-permute-start | bytes 12441608 | tf_op jit(solution)/shard_map/ppermute | solution.py:36
  23.9 20.9 %collective-permute-start.3 = (bf16[2,64,2880]{2,1,0:T(8,128)(2,1)}, bf16[2,64,2880]{2,1,0:T(8,128)(2,1)S(1)}, u32[]{:S(2)}, u32[]{:S(2)}) collective-permute-start(bf16[2,64,2880]{2,1,0:T(8,128)(2,1)} %get-tuple-element.82.refs_5_), channel_id=1, source_target_pairs={{0,24},{8,16},{16,8},{24,0},{1,25},{9,17},{17,9},{25,1},{2,26},{10... | collective-permute-start | bytes 2211848 | tf_op jit(solution)/shard_map/ppermute | solution.py:24
  25.5 34.4 %collective-permute-start.4 = (bf16[2,64,2880]{2,1,0:T(8,128)(2,1)}, bf16[2,64,2880]{2,1,0:T(8,128)(2,1)S(1)}, u32[]{:S(2)}, u32[]{:S(2)}) collective-permute-start(bf16[2,64,2880]{2,1,0:T(8,128)(2,1)} %get-tuple-element.83), channel_id=1, source_target_pairs={{0,16},{8,24},{16,0},{24,8},{1,17},{9,25},{17,1},{25,9},{2,18},{10... | collective-permute-start | bytes 2211848 | tf_op jit(solution)/shard_map/ppermute | solution.py:24
  26.6 33.4 %collective-permute-start.5 = (bf16[2,64,2880]{2,1,0:T(8,128)(2,1)}, bf16[2,64,2880]{2,1,0:T(8,128)(2,1)S(1)}, u32[]{:S(2)}, u32[]{:S(2)}) collective-permute-start(bf16[2,64,2880]{2,1,0:T(8,128)(2,1)} %get-tuple-element.84), channel_id=1, source_target_pairs={{0,8},{8,0},{16,24},{24,16},{1,9},{9,1},{17,25},{25,17},{2,10},{10... | collective-permute-start | bytes 2211848 | tf_op jit(solution)/shard_map/ppermute | solution.py:24
  34.4 1.4 copy-start
  35.8 2.7 %copy-start.1 = (f32[2,64,2880]{2,1,0:T(8,128)S(1)}, f32[2,64,2880]{2,1,0:T(8,128)}, u32[]{:S(2)}) copy-start(f32[2,64,2880]{2,1,0:T(8,128)} %shard_map.111.refs_0_) | copy-start | bytes 4423684
  35.8 53.7 %slice-start.3 = ((s8[4239360]{0:T(1024)(128)(4,1)}), s8[4194304]{0:T(1024)(128)(4,1)S(1)}, s32[]{:S(2)}) async-start(s8[4239360]{0:T(1024)(128)(4,1)} %bitcast.32), calls=%async_computation.3 | async-start | bytes 8388608
  38.4 51.0 %slice-start.4 = ((s8[4239360]{0:T(1024)(128)(4,1)}), s8[45056]{0:T(1024)(128)(4,1)S(1)}, s32[]{:S(2)}) async-start(s8[4239360]{0:T(1024)(128)(4,1)} %bitcast.32), calls=%async_computation.4 | async-start | bytes 90112
  38.5 51.0 %slice-start = ((s8[8478720]{0:T(1024)(128)(4,1)}), s8[4194304]{0:T(1024)(128)(4,1)S(1)}, s32[]{:S(2)}) async-start(s8[8478720]{0:T(1024)(128)(4,1)} %bitcast.25), calls=%async_computation | async-start | bytes 8388608
  38.5 51.0 %slice-start.1 = ((s8[8478720]{0:T(1024)(128)(4,1)}), s8[4194304]{0:T(1024)(128)(4,1)S(1)}, s32[]{:S(2)}) async-start(s8[8478720]{0:T(1024)(128)(4,1)} %bitcast.25), calls=%async_computation.1 | async-start | bytes 8388608
  42.8 46.7 %slice-start.2 = ((s8[8478720]{0:T(1024)(128)(4,1)}), s8[90112]{0:T(1024)(128)(4,1)S(1)}, s32[]{:S(2)}) async-start(s8[8478720]{0:T(1024)(128)(4,1)} %bitcast.25), calls=%async_computation.2 | async-start | bytes 180224
  61.9 20.8 %collective-permute-start.11 = (bf16[2,64,2944]{2,1,0:T(8,128)(2,1)S(1)}, bf16[2,64,2944]{2,1,0:T(8,128)(2,1)S(1)}, u32[]{:S(2)}, u32[]{:S(2)}) collective-permute-start(bf16[2,64,2944]{2,1,0:T(8,128)(2,1)S(1)} %get-tuple-element.92), channel_id=1, source_target_pairs={{0,2},{1,3},{2,4},{3,5},{4,6},{5,7},{6,0},{7,1},{8,10},{9,11},{10,... | collective-permute-start | bytes 2261000 | tf_op jit(solution)/shard_map/ppermute | solution.py:31
  63.5 11.7 %collective-permute-start.8 = (bf16[64,2880]{1,0:T(8,128)(2,1)S(1)}, bf16[64,2880]{1,0:T(8,128)(2,1)S(1)}, u32[]{:S(2)}, u32[]{:S(2)}) collective-permute-start(bf16[64,2880]{1,0:T(8,128)(2,1)S(1)} %get-tuple-element.89), channel_id=1, source_target_pairs={{0,8},{8,0},{16,24},{24,16},{1,9},{9,1},{17,25},{25,17},{2,10},{10... | collective-permute-start | bytes 1105928 | tf_op jit(solution)/shard_map/ppermute | solution.py:24
  64.5 18.2 %collective-permute-start.9 = (bf16[64,2880]{1,0:T(8,128)(2,1)S(1)}, bf16[64,2880]{1,0:T(8,128)(2,1)S(1)}, u32[]{:S(2)}, u32[]{:S(2)}) collective-permute-start(bf16[64,2880]{1,0:T(8,128)(2,1)S(1)} %get-tuple-element.90), channel_id=1, source_target_pairs={{0,16},{8,24},{16,0},{24,8},{1,17},{9,25},{17,1},{25,9},{2,18},{10... | collective-permute-start | bytes 1105928 | tf_op jit(solution)/shard_map/ppermute | solution.py:24
  65.5 17.3 %collective-permute-start.10 = (bf16[64,2880]{1,0:T(8,128)(2,1)S(1)}, bf16[64,2880]{1,0:T(8,128)(2,1)S(1)}, u32[]{:S(2)}, u32[]{:S(2)}) collective-permute-start(bf16[64,2880]{1,0:T(8,128)(2,1)S(1)} %get-tuple-element.91), channel_id=1, source_target_pairs={{0,24},{8,16},{16,8},{24,0},{1,25},{9,17},{17,9},{25,1},{2,26},{10... | collective-permute-start | bytes 1105928 | tf_op jit(solution)/shard_map/ppermute | solution.py:24
  84.2 19.6 %collective-permute-start.12 = (bf16[2,64,2944]{2,1,0:T(8,128)(2,1)S(1)}, bf16[2,64,2944]{2,1,0:T(8,128)(2,1)S(1)}, u32[]{:S(2)}, u32[]{:S(2)}) collective-permute-start(bf16[2,64,2944]{2,1,0:T(8,128)(2,1)S(1)} %collective-permute-done.11.held_ref), channel_id=1, source_target_pairs={{0,2},{1,3},{2,4},{3,5},{4,6},{5,7},{6,0},{7,1},{8,10},{9,11},{10,... | collective-permute-start | bytes 2261000 | tf_op jit(solution)/shard_map/ppermute | solution.py:31
  86.0 12.6 %collective-permute-start.13 = (bf16[64,2880]{1,0:T(8,128)(2,1)S(1)}, bf16[64,2880]{1,0:T(8,128)(2,1)S(1)}, u32[]{:S(2)}, u32[]{:S(2)}) collective-permute-start(bf16[64,2880]{1,0:T(8,128)(2,1)S(1)} %get-tuple-element.103), channel_id=1, source_target_pairs={{0,8},{8,0},{16,24},{24,16},{1,9},{9,1},{17,25},{25,17},{2,10},{10... | collective-permute-start | bytes 1105928 | tf_op jit(solution)/shard_map/ppermute | solution.py:24
  86.9 16.8 %collective-permute-start.14 = (bf16[64,2880]{1,0:T(8,128)(2,1)S(1)}, bf16[64,2880]{1,0:T(8,128)(2,1)S(1)}, u32[]{:S(2)}, u32[]{:S(2)}) collective-permute-start(bf16[64,2880]{1,0:T(8,128)(2,1)S(1)} %get-tuple-element.104), channel_id=1, source_target_pairs={{0,16},{8,24},{16,0},{24,8},{1,17},{9,25},{17,1},{25,9},{2,18},{10... | collective-permute-start | bytes 1105928 | tf_op jit(solution)/shard_map/ppermute | solution.py:24
  88.1 15.6 %collective-permute-start.15 = (bf16[64,2880]{1,0:T(8,128)(2,1)S(1)}, bf16[64,2880]{1,0:T(8,128)(2,1)S(1)}, u32[]{:S(2)}, u32[]{:S(2)}) collective-permute-start(bf16[64,2880]{1,0:T(8,128)(2,1)S(1)} %get-tuple-element.105), channel_id=1, source_target_pairs={{0,24},{8,16},{16,8},{24,0},{1,25},{9,17},{17,9},{25,1},{2,26},{10... | collective-permute-start | bytes 1105928 | tf_op jit(solution)/shard_map/ppermute | solution.py:24
  105.2 21.9 %collective-permute-start.16 = (bf16[2,64,2944]{2,1,0:T(8,128)(2,1)S(1)}, bf16[2,64,2944]{2,1,0:T(8,128)(2,1)S(1)}, u32[]{:S(2)}, u32[]{:S(2)}) collective-permute-start(bf16[2,64,2944]{2,1,0:T(8,128)(2,1)S(1)} %collective-permute-done.12.held_ref), channel_id=1, source_target_pairs={{0,2},{1,3},{2,4},{3,5},{4,6},{5,7},{6,0},{7,1},{8,10},{9,11},{10,... | collective-permute-start | bytes 2261000 | tf_op jit(solution)/shard_map/ppermute | solution.py:31
  106.8 13.7 %collective-permute-start.17 = (bf16[64,2880]{1,0:T(8,128)(2,1)S(1)}, bf16[64,2880]{1,0:T(8,128)(2,1)S(1)}, u32[]{:S(2)}, u32[]{:S(2)}) collective-permute-start(bf16[64,2880]{1,0:T(8,128)(2,1)S(1)} %get-tuple-element.111), channel_id=1, source_target_pairs={{0,8},{8,0},{16,24},{24,16},{1,9},{9,1},{17,25},{25,17},{2,10},{10... | collective-permute-start | bytes 1105928 | tf_op jit(solution)/shard_map/ppermute | solution.py:24
  107.8 13.5 %collective-permute-start.18 = (bf16[64,2880]{1,0:T(8,128)(2,1)S(1)}, bf16[64,2880]{1,0:T(8,128)(2,1)S(1)}, u32[]{:S(2)}, u32[]{:S(2)}) collective-permute-start(bf16[64,2880]{1,0:T(8,128)(2,1)S(1)} %get-tuple-element.112), channel_id=1, source_target_pairs={{0,16},{8,24},{16,0},{24,8},{1,17},{9,25},{17,1},{25,9},{2,18},{10... | collective-permute-start | bytes 1105928 | tf_op jit(solution)/shard_map/ppermute | solution.py:24
  108.7 18.4 %collective-permute-start.19 = (bf16[64,2880]{1,0:T(8,128)(2,1)S(1)}, bf16[64,2880]{1,0:T(8,128)(2,1)S(1)}, u32[]{:S(2)}, u32[]{:S(2)}) collective-permute-start(bf16[64,2880]{1,0:T(8,128)(2,1)S(1)} %get-tuple-element.113), channel_id=1, source_target_pairs={{0,24},{8,16},{16,8},{24,0},{1,25},{9,17},{17,9},{25,1},{2,26},{10... | collective-permute-start | bytes 1105928 | tf_op jit(solution)/shard_map/ppermute | solution.py:24
  119.4 20.3 %collective-permute-start.23 = (bf16[64,2880]{1,0:T(8,128)(2,1)S(1)}, bf16[64,2880]{1,0:T(8,128)(2,1)S(1)}, u32[]{:S(2)}, u32[]{:S(2)}) collective-permute-start(bf16[64,2880]{1,0:T(8,128)(2,1)S(1)} %get-tuple-element.125), channel_id=1, source_target_pairs={{0,8},{8,0},{16,24},{24,16},{1,9},{9,1},{17,25},{25,17},{2,10},{10... | collective-permute-start | bytes 1105928 | tf_op jit(solution)/shard_map/ppermute | solution.py:24
  120.5 19.8 %collective-permute-start.24 = (bf16[64,2880]{1,0:T(8,128)(2,1)S(1)}, bf16[64,2880]{1,0:T(8,128)(2,1)S(1)}, u32[]{:S(2)}, u32[]{:S(2)}) collective-permute-start(bf16[64,2880]{1,0:T(8,128)(2,1)S(1)} %get-tuple-element.126), channel_id=1, source_target_pairs={{0,16},{8,24},{16,0},{24,8},{1,17},{9,25},{17,1},{25,9},{2,18},{10... | collective-permute-start | bytes 1105928 | tf_op jit(solution)/shard_map/ppermute | solution.py:24
  121.3 21.9 %collective-permute-start.25 = (bf16[64,2880]{1,0:T(8,128)(2,1)S(1)}, bf16[64,2880]{1,0:T(8,128)(2,1)S(1)}, u32[]{:S(2)}, u32[]{:S(2)}) collective-permute-start(bf16[64,2880]{1,0:T(8,128)(2,1)S(1)} %get-tuple-element.127), channel_id=1, source_target_pairs={{0,24},{8,16},{16,8},{24,0},{1,25},{9,17},{17,9},{25,1},{2,26},{10... | collective-permute-start | bytes 1105928 | tf_op jit(solution)/shard_map/ppermute | solution.py:24
  128.5 22.1 %collective-permute-start.20 = (bf16[64,2880]{1,0:T(8,128)(2,1)S(1)}, bf16[64,2880]{1,0:T(8,128)(2,1)S(1)}, u32[]{:S(2)}, u32[]{:S(2)}) collective-permute-start(bf16[64,2880]{1,0:T(8,128)(2,1)S(1)} %get-tuple-element.121), channel_id=1, source_target_pairs={{0,8},{8,0},{16,24},{24,16},{1,9},{9,1},{17,25},{25,17},{2,10},{10... | collective-permute-start | bytes 1105928 | tf_op jit(solution)/shard_map/ppermute | solution.py:24
  129.4 22.5 %collective-permute-start.21 = (bf16[64,2880]{1,0:T(8,128)(2,1)S(1)}, bf16[64,2880]{1,0:T(8,128)(2,1)S(1)}, u32[]{:S(2)}, u32[]{:S(2)}) collective-permute-start(bf16[64,2880]{1,0:T(8,128)(2,1)S(1)} %get-tuple-element.122), channel_id=1, source_target_pairs={{0,16},{8,24},{16,0},{24,8},{1,17},{9,25},{17,1},{25,9},{2,18},{10... | collective-permute-start | bytes 1105928 | tf_op jit(solution)/shard_map/ppermute | solution.py:24
  143.6 32.9 %collective-permute-start.35 = (bf16[2,64,2880]{2,1,0:T(8,128)(2,1)S(1)}, bf16[2,64,2880]{2,1,0:T(8,128)(2,1)S(1)}, u32[]{:S(2)}, u32[]{:S(2)}) collective-permute-start(bf16[2,64,2880]{2,1,0:T(8,128)(2,1)S(1)} %shard_map.121.refs_8_), channel_id=1, source_target_pairs={{0,2},{1,3},{2,4},{3,5},{4,6},{5,7},{6,0},{7,1},{8,10},{9,11},{10,... | collective-permute-start | bytes 2211848 | tf_op jit(solution)/shard_map/ppermute | solution.py:31
  144.4 32.1 %collective-permute-start.32 = (bf16[64,2880]{1,0:T(8,128)(2,1)S(1)}, bf16[64,2880]{1,0:T(8,128)(2,1)S(1)}, u32[]{:S(2)}, u32[]{:S(2)}) collective-permute-start(bf16[64,2880]{1,0:T(8,128)(2,1)S(1)} %get-tuple-element.129.refs_5_), channel_id=1, source_target_pairs={{0,8},{8,0},{16,24},{24,16},{1,9},{9,1},{17,25},{25,17},{2,10},{10... | collective-permute-start | bytes 1105928 | tf_op jit(solution)/shard_map/ppermute | solution.py:24
  145.2 22.2 %collective-permute-start.22 = (bf16[64,2880]{1,0:T(8,128)(2,1)S(1)}, bf16[64,2880]{1,0:T(8,128)(2,1)S(1)}, u32[]{:S(2)}, u32[]{:S(2)}) collective-permute-start(bf16[64,2880]{1,0:T(8,128)(2,1)S(1)} %get-tuple-element.123), channel_id=1, source_target_pairs={{0,24},{8,16},{16,8},{24,0},{1,25},{9,17},{17,9},{25,1},{2,26},{10... | collective-permute-start | bytes 1105928 | tf_op jit(solution)/shard_map/ppermute | solution.py:24
  150.6 25.9 %collective-permute-start.33 = (bf16[64,2880]{1,0:T(8,128)(2,1)S(1)}, bf16[64,2880]{1,0:T(8,128)(2,1)S(1)}, u32[]{:S(2)}, u32[]{:S(2)}) collective-permute-start(bf16[64,2880]{1,0:T(8,128)(2,1)S(1)} %get-tuple-element.130.refs_6_), channel_id=1, source_target_pairs={{0,16},{8,24},{16,0},{24,8},{1,17},{9,25},{17,1},{25,9},{2,18},{10... | collective-permute-start | bytes 1105928 | tf_op jit(solution)/shard_map/ppermute | solution.py:24
  151.9 24.7 %collective-permute-start.34 = (bf16[64,2880]{1,0:T(8,128)(2,1)S(1)}, bf16[64,2880]{1,0:T(8,128)(2,1)S(1)}, u32[]{:S(2)}, u32[]{:S(2)}) collective-permute-start(bf16[64,2880]{1,0:T(8,128)(2,1)S(1)} %get-tuple-element.131.refs_7_), channel_id=1, source_target_pairs={{0,24},{8,16},{16,8},{24,0},{1,25},{9,17},{17,9},{25,1},{2,26},{10... | collective-permute-start | bytes 1105928 | tf_op jit(solution)/shard_map/ppermute | solution.py:24
  177.0 16.9 %collective-permute-start.36 = (bf16[2,64,2880]{2,1,0:T(8,128)(2,1)S(1)}, bf16[2,64,2880]{2,1,0:T(8,128)(2,1)S(1)}, u32[]{:S(2)}, u32[]{:S(2)}) collective-permute-start(bf16[2,64,2880]{2,1,0:T(8,128)(2,1)S(1)} %shard_map.123.refs_5_), channel_id=1, source_target_pairs={{0,2},{1,3},{2,4},{3,5},{4,6},{5,7},{6,0},{7,1},{8,10},{9,11},{10,... | collective-permute-start | bytes 2211848 | tf_op jit(solution)/shard_map/ppermute | solution.py:31
  177.6 7.6 %collective-permute-start.29 = (bf16[64,2880]{1,0:T(8,128)(2,1)S(1)}, bf16[64,2880]{1,0:T(8,128)(2,1)S(1)}, u32[]{:S(2)}, u32[]{:S(2)}) collective-permute-start(bf16[64,2880]{1,0:T(8,128)(2,1)S(1)} %get-tuple-element.133.refs_6_), channel_id=1, source_target_pairs={{0,8},{8,0},{16,24},{24,16},{1,9},{9,1},{17,25},{25,17},{2,10},{10... | collective-permute-start | bytes 1105928 | tf_op jit(solution)/shard_map/ppermute | solution.py:24
  178.4 10.0 %collective-permute-start.30 = (bf16[64,2880]{1,0:T(8,128)(2,1)S(1)}, bf16[64,2880]{1,0:T(8,128)(2,1)S(1)}, u32[]{:S(2)}, u32[]{:S(2)}) collective-permute-start(bf16[64,2880]{1,0:T(8,128)(2,1)S(1)} %get-tuple-element.134.refs_7_), channel_id=1, source_target_pairs={{0,16},{8,24},{16,0},{24,8},{1,17},{9,25},{17,1},{25,9},{2,18},{10... | collective-permute-start | bytes 1105928 | tf_op jit(solution)/shard_map/ppermute | solution.py:24
  179.6 13.1 %collective-permute-start.31 = (bf16[64,2880]{1,0:T(8,128)(2,1)S(1)}, bf16[64,2880]{1,0:T(8,128)(2,1)S(1)}, u32[]{:S(2)}, u32[]{:S(2)}) collective-permute-start(bf16[64,2880]{1,0:T(8,128)(2,1)S(1)} %get-tuple-element.135.refs_8_), channel_id=1, source_target_pairs={{0,24},{8,16},{16,8},{24,0},{1,25},{9,17},{17,9},{25,1},{2,26},{10... | collective-permute-start | bytes 1105928 | tf_op jit(solution)/shard_map/ppermute | solution.py:24
  194.2 13.5 %collective-permute-start.37 = (bf16[2,64,2880]{2,1,0:T(8,128)(2,1)S(1)}, bf16[2,64,2880]{2,1,0:T(8,128)(2,1)S(1)}, u32[]{:S(2)}, u32[]{:S(2)}) collective-permute-start(bf16[2,64,2880]{2,1,0:T(8,128)(2,1)S(1)} %shard_map.124.refs_5_), channel_id=1, source_target_pairs={{0,2},{1,3},{2,4},{3,5},{4,6},{5,7},{6,0},{7,1},{8,10},{9,11},{10,... | collective-permute-start | bytes 2211848 | tf_op jit(solution)/shard_map/ppermute | solution.py:31
  194.4 7.6 %collective-permute-start.26 = (bf16[64,2880]{1,0:T(8,128)(2,1)S(1)}, bf16[64,2880]{1,0:T(8,128)(2,1)S(1)}, u32[]{:S(2)}, u32[]{:S(2)}) collective-permute-start(bf16[64,2880]{1,0:T(8,128)(2,1)S(1)} %get-tuple-element.137), channel_id=1, source_target_pairs={{0,8},{8,0},{16,24},{24,16},{1,9},{9,1},{17,25},{25,17},{2,10},{10... | collective-permute-start | bytes 1105928 | tf_op jit(solution)/shard_map/ppermute | solution.py:24
  195.7 11.6 %collective-permute-start.27 = (bf16[64,2880]{1,0:T(8,128)(2,1)S(1)}, bf16[64,2880]{1,0:T(8,128)(2,1)S(1)}, u32[]{:S(2)}, u32[]{:S(2)}) collective-permute-start(bf16[64,2880]{1,0:T(8,128)(2,1)S(1)} %get-tuple-element.138), channel_id=1, source_target_pairs={{0,16},{8,24},{16,0},{24,8},{1,17},{9,25},{17,1},{25,9},{2,18},{10... | collective-permute-start | bytes 1105928 | tf_op jit(solution)/shard_map/ppermute | solution.py:24
  196.4 10.9 %collective-permute-start.28 = (bf16[64,2880]{1,0:T(8,128)(2,1)S(1)}, bf16[64,2880]{1,0:T(8,128)(2,1)S(1)}, u32[]{:S(2)}, u32[]{:S(2)}) collective-permute-start(bf16[64,2880]{1,0:T(8,128)(2,1)S(1)} %get-tuple-element.139), channel_id=1, source_target_pairs={{0,24},{8,16},{16,8},{24,0},{1,25},{9,17},{17,9},{25,1},{2,26},{10... | collective-permute-start | bytes 1105928 | tf_op jit(solution)/shard_map/ppermute | solution.py:24
where the time goes:
time: 210 us; the launch traced here: 209 us
  waiting for transfers between devices  93.8 us (45%)
  Pallas kernels  68.4 us (33%)
  starting transfers between devices  43.5 us (21%)
  local copies, waits for them, and re-layouts  2.88 us (1%)
    ppermute x30, waiting for transfers between devices, ctx_swap(): return lax.ppermute(rows, 'ctx', [(i, i ^ distance) for i in range(count)])  92.5 us
    pallas_call x4, Pallas kernels, expert(): pl.pallas_call(functools.partial(expert_kernel, ctx_count, tile), out_sha...  36.3 us
    ppermute x30, starting transfers between devices, ctx_swap(): return lax.ppermute(rows, 'ctx', [(i, i ^ distance) for i in range(count)])  36.3 us
    pallas_call x2, Pallas kernels, attend(): pl.pallas_call(functools.partial(attend_kernel, dests, ctx_count), out_sh...  15.3 us
    pallas_call x2, Pallas kernels, copy_after(): pl.pallas_call(copy_kernel, out_shape=jax.ShapeDtypeStruct(source.shape,...  6.91 us
    ppermute x6, starting transfers between devices, plane_shift(): lax.ppermute(rows, 'exp', [(i, (i + 2 * planes) % count) for i in range(c...  6.65 us
    pallas_call x3, Pallas kernels, pick_rows(): pl.pallas_call(functools.partial(pick_kernel, ctx_count), out_shape=pick_...  4.31 us
  transfers between devices with their start and end apart: 38, of which 20 were waited for; matrix products, arithmetic and copies ran while one was open for 0% of the time, Pallas kernels for 29%

commit v1 on v0

--- a/solution.py
+++ b/solution.py
@@ -120,7 +120,7 @@
 
 def attend_kernel(dests, ctx_count, ctx_ref, order_ref, weight_ref, *refs):
     out_refs, (weight_buf, got_refs, sems) = refs[-3 - len(dests) : -3], refs[-3:]
-    hidden_ref = refs[ctx_count]
+    hidden_ref, arrived_ref = refs[ctx_count : ctx_count + 2]
     copies = start_copies([(refs[d], got_refs.at[d]) for d in range(ctx_count)], sems)
     weight_copy = start_copies([(weight_ref, weight_buf)], sems, ctx_count)[0]
     for copy in copies:
@@ -174,24 +174,24 @@
         if d == 0:
             eye = lax.broadcasted_iota(jnp.int32, (rows, rows), 1) == row
             part = part + nt_dot(eye.astype(jnp.bfloat16), hidden_ref[...])
+            part = part + merged(arrived_ref[...]).astype(jnp.float32)
         out_ref[...] = part.astype(out_ref.dtype).reshape(out_ref.shape)
 
 
-def attend(dests, ctx_scalar, order, weight, got, hidden, after):
+def attend(dests, ctx_scalar, order, weight, got, added, after):
     ctx_count = len(got)
     rows, columns = got[0].shape[0], weight.shape[0]
     shapes = [
         jax.ShapeDtypeStruct((2, rows // 2, columns), jnp.bfloat16 if d else jnp.float32)
         for d in dests
     ]
-    extra = [hidden] if 0 in dests else []
     work = len(dests) * rows * weight.shape[1]
     return pl.pallas_call(
         functools.partial(attend_kernel, dests, ctx_count),
         out_shape=shapes,
         in_specs=[SMEM_SPEC, SMEM_SPEC]
         + [ANY_SPEC] * (1 + ctx_count)
-        + [VMEM_SPEC] * len(extra)
+        + [VMEM_SPEC] * len(added)
         + [ANY_SPEC] * len(after),
         out_specs=[VMEM_SPEC] * len(dests),
         scratch_shapes=[
@@ -201,7 +201,7 @@
         ],
         compiler_params=pltpu.CompilerParams(vmem_limit_bytes=56 << 20),
         cost_estimate=SMALL_COST,
-    )(ctx_scalar, order, weight, *got, *extra, *after)
+    )(ctx_scalar, order, weight, *got, *added, *after)
 
 
 def pick_and_mix(ctx_count, capacity, ctx_ref, plane_ref, held, route, out_refs, mix_ref):
@@ -227,9 +227,9 @@
         out_ref[...] = picked[d * capacity : (d + 1) * capacity]
 
 
-def norm_kernel(part_count, ctx_ref, plane_ref, gain_ref, route_ref, *refs):
+def norm_kernel(ctx_count, part_count, ctx_ref, plane_ref, gain_ref, route_ref, *refs):
     part_refs = refs[:part_count]
-    residual_ref, normed_ref, mix_ref, *out_refs = refs[-3 - part_count :]
+    residual_ref, normed_ref, mix_ref, *out_refs = refs[-3 - ctx_count :]
     capacity, columns = out_refs[0].shape
     total = merged(part_refs[0][...])
     for part_ref in part_refs[1:]:
@@ -243,7 +243,7 @@
     normed_ref[:, :, :columns] = normed.reshape(residual_ref.shape)
     normed_ref[:, :, columns:] = route.reshape(normed_ref.shape[:2] + route.shape[1:])
     pick_and_mix(
-        part_count,
+        ctx_count,
         capacity,
         ctx_ref,
         plane_ref,
@@ -259,18 +259,18 @@
     return [jax.ShapeDtypeStruct((tokens, ctx_count * capacity), jnp.bfloat16)] + [slot] * ctx_count
 
 
-def norm_and_pick(ctx_scalar, plane_scalars, gain, route, parts, capacity, after):
+def norm_and_pick(ctx_scalar, plane_scalars, gain, route, parts, ctx_count, capacity, after):
     _, half, columns = parts[0].shape
     tokens, extra = route.shape
     return pl.pallas_call(
-        functools.partial(norm_kernel, len(parts)),
+        functools.partial(norm_kernel, ctx_count, len(parts)),
         out_shape=[
             jax.ShapeDtypeStruct((2, half, columns), jnp.bfloat16),
             jax.ShapeDtypeStruct((2, half, columns + extra), jnp.bfloat16),
         ]
-        + pick_shapes(len(parts), capacity, tokens, columns),
+        + pick_shapes(ctx_count, capacity, tokens, columns),
         in_specs=[SMEM_SPEC] * 2 + [VMEM_SPEC] * (2 + len(parts)) + [ANY_SPEC] * len(after),
-        out_specs=[VMEM_SPEC] * (3 + len(parts)),
+        out_specs=[VMEM_SPEC] * (3 + ctx_count),
         compiler_params=pltpu.CompilerParams(vmem_limit_bytes=12 << 20),
         cost_estimate=SMALL_COST,
     )(ctx_scalar, plane_scalars, gain, route, *parts, *after)
@@ -329,10 +329,10 @@
         out_ref[...] = total_ref[d * capacity : (d + 1) * capacity].astype(jnp.bfloat16)
 
 
-def expert(rows, gate_ups, downs, after):
+def expert(rows, gate_ups, downs, after, tiles):
     ctx_count = len(rows)
     capacity, columns = rows[0].shape
-    tile = downs[0].shape[0] // 3
+    tile = downs[0].shape[0] // tiles
     return pl.pallas_call(
         functools.partial(expert_kernel, ctx_count, tile),
         out_shape=[jax.ShapeDtypeStruct((capacity, columns), jnp.bfloat16)] * ctx_count,
@@ -418,12 +418,14 @@
     got, gate_up_mine, down_mine = lax.optimization_barrier((got, gate_up_mine, down_mine))
 
     weight = jnp.swapaxes(out_weight, 0, 1)
-    partners = tuple(range(last, 0, -1))
-    parts = list(attend(partners, ctx_scalar, block_order, weight, got, None, []))
+    first = list(attend((last,), ctx_scalar, block_order, weight, got, [], []))
+    partners = tuple(range(last - 1, 0, -1))
+    parts = list(attend(partners, ctx_scalar, block_order, weight, got, [], first))
     swapped = [core_swap(gate_up_mine), core_swap(down_mine)]
     hidden_columns = jnp.swapaxes(hidden[0], 0, 1)
-    own = attend((0,), ctx_scalar, block_order, weight, got, hidden_columns, parts[:1])
-    parts = [ctx_swap(part, last - i) for i, part in enumerate(parts)]
+    added = [hidden_columns, ctx_swap(first[0], last)]
+    own = attend((0,), ctx_scalar, block_order, weight, got, added, parts[:1])
+    parts = [ctx_swap(part, partners[i]) for i, part in enumerate(parts)]
     other = [copy_after(w, list(own)) for w in swapped]
     gate_ups = [w.reshape(2, half, D) for w in (gate_up_mine, other[0])]
     downs = [down_mine, other[1]]
@@ -433,7 +435,14 @@
     )
     route = jnp.pad(route, ((0, 0), (0, -D % 128 - 2 * TOPK)))
     residual, held, mix, *rows = norm_and_pick(
-        ctx_scalar, plane_scalars, norm_gain[None], route, list(own) + parts, capacity, other
+        ctx_scalar,
+        plane_scalars,
+        norm_gain[None],
+        route,
+        list(own) + parts,
+        ctx_count,
+        capacity,
+        other,
     )
 
     def spread(blocks):
@@ -444,7 +453,7 @@
     back = [None] * planes
 
     def run_expert(s, after):
-        result = expert(arrived[s], gate_ups, downs, after)
+        result = expert(arrived[s], gate_ups, downs, after, 1 if s == planes - 1 else 3)
         if s > 0:
             back[s] = spread(result)
         return list(result)

time: 210 us -> 203 us (0.967)
  waiting for transfers between devices: 93.8 us -> 83.9 us
    ppermute x30, waiting for transfers between devices: 92.5 us -> 82 us  [ctx_swap(): return lax.ppermute(rows, 'ctx', [(i, i ^ distance) for i in range(count)])]
    pallas_call x2 -> x3, Pallas kernels: 15.3 us -> 18.8 us  [attend(): pl.pallas_call(functools.partial(attend_kernel, dests, ctx_count), out_sh...]
  transfers between devices with their start and end apart: 38 -> 38, of which waited for: 20 -> 19; matrix products, arithmetic and copies ran while one was open for 0% -> 0% of each run, Pallas kernels for 29% -> 31%
where the time goes in v1:
time: 203 us
  waiting for transfers between devices  83.9 us (41%)
  Pallas kernels  70.4 us (35%)
  starting transfers between devices  44.3 us (22%)
  local copies, waits for them, and re-layouts  3.76 us (2%)
    ppermute x30, waiting for transfers between devices, ctx_swap(): return lax.ppermute(rows, 'ctx', [(i, i ^ distance) for i in range(count)])  82 us
    ppermute x30, starting transfers between devices, ctx_swap(): return lax.ppermute(rows, 'ctx', [(i, i ^ distance) for i in range(count)])  35.1 us
    pallas_call x4, Pallas kernels, expert(): pl.pallas_call(functools.partial(expert_kernel, ctx_count, tile), out_sha...  34.9 us
    pallas_call x3, Pallas kernels, attend(): pl.pallas_call(functools.partial(attend_kernel, dests, ctx_count), out_sh...  18.8 us
    ppermute x6, starting transfers between devices, plane_shift(): lax.ppermute(rows, 'exp', [(i, (i + 2 * planes) % count) for i in range(c...  8.68 us
    pallas_call x2, Pallas kernels, copy_after(): pl.pallas_call(copy_kernel, out_shape=jax.ShapeDtypeStruct(source.shape,...  6.91 us
    pallas_call x3, Pallas kernels, pick_rows(): pl.pallas_call(functools.partial(pick_kernel, ctx_count), out_shape=pick_...  4.31 us
  transfers between devices with their start and end apart: 38, of which 19 were waited for; matrix products, arithmetic and copies ran while one was open for 0% of the time, Pallas kernels for 31%

profile of v1, /device:TPU:0, one launch (start us, length us, event | category | flops | bytes accessed | tf_op | source)
XLA Modules:
  0.0 202.9 jit_solution(1804526673293852112)
XLA Ops:
  0.0 2.1 %shard_map.109 = (bf16[128,640]{1,0:T(8,128)(2,1)}, bf16[128,640]{1,0:T(8,128)(2,1)}, bf16[128,640]{1,0:T(8,128)(2,1)}, bf16[128,640]{1,0:T(8,128)(2,1)}) custom-call(s32[1]{0:T(128)} %bitcast.ctx_ref, bf16[128,2048]{1,0:T(8,128)(2,1)} %bitcast.43, bf16[128,256]{1,0:T(8,128)(2,1)} %bitcast.44, bf16[128,256]{1,0:T(8,128)(2,1)} %bitcast.45), custom_call_target="tpu_custom_call" | custom-call | flops 1 | bytes 1 | tf_op jit(solution)/shard_map/pallas_call | solution.py:94
  2.1 3.0 %collective-permute-start = (bf16[128,640]{1,0:T(8,128)(2,1)}, bf16[128,640]{1,0:T(8,128)(2,1)S(1)}, u32[]{:S(2)}, u32[]{:S(2)}) collective-permute-start(bf16[128,640]{1,0:T(8,128)(2,1)} %get-tuple-element.74), channel_id=1, source_target_pairs={{0,8},{8,0},{16,24},{24,16},{1,9},{9,1},{17,25},{25,17},{2,10},{10... | collective-permute-start | bytes 491528 | tf_op jit(solution)/shard_map/ppermute | solution.py:24
  5.1 1.5 collective-permute-start.1
  6.6 3.7 %collective-permute-done.refs_1_ = bf16[128,640]{1,0:T(8,128)(2,1)S(1)} collective-permute-done((bf16[128,640]{1,0:T(8,128)(2,1)}, bf16[128,640]{1,0:T(8,128)(2,1)S(1)}, u32[]{:S(2)}, u32[]{:S(2)}) %collective-permute-start) | collective-permute-done | bytes 163872 | tf_op jit(solution)/shard_map/ppermute | solution.py:24
  10.3 4.1 %collective-permute-done.1.refs_2_ = bf16[128,640]{1,0:T(8,128)(2,1)S(1)} collective-permute-done((bf16[128,640]{1,0:T(8,128)(2,1)}, bf16[128,640]{1,0:T(8,128)(2,1)S(1)}, u32[]{:S(2)}, u32[]{:S(2)}) %collective-permute-start.1) | collective-permute-done | bytes 163872 | tf_op jit(solution)/shard_map/ppermute | solution.py:24
  15.2 5.3 %shard_map.110.refs_4_ = bf16[2,64,2880]{2,1,0:T(8,128)(2,1)} custom-call(s32[1]{0:T(128)} %bitcast.ctx_ref, s32[8]{0:T(128)} %order_ref.5, bf16[2880,512]{1,0:T(8,128)(2,1)} %bitcast.39, bf16[128,640]{1,0:T(8,128)(2,1)} %get-tuple-element.77.refs_0_, bf16[128,640]{1,0:T(8,128)(2,1)} %copy-done.2, bf16[128,640]{1,0:T(8,128)(2,1)} %copy-done.3, ...), custom_call_target="tpu_custom_call" | custom-call | flops 1 | bytes 1 | tf_op jit(solution)/shard_map/pallas_call | solution.py:189
  20.5 1.6 collective-permute-start.3
  22.0 6.7 %shard_map.111 = (bf16[2,64,2880]{2,1,0:T(8,128)(2,1)}, bf16[2,64,2880]{2,1,0:T(8,128)(2,1)}) custom-call(s32[1]{0:T(128)} %bitcast.ctx_ref, s32[8]{0:T(128)} %order_ref.5, bf16[2880,512]{1,0:T(8,128)(2,1)} %bitcast.40, bf16[128,640]{1,0:T(8,128)(2,1)} %get-tuple-element.77.refs_0_, bf16[128,640]{1,0:T(8,128)(2,1)} %copy-done.2, bf16[128,640]{1,0:T(8,128)(2,1)} %copy-done.3, ...), custom_call_target="tpu_custom_call" | custom-call | flops 1 | bytes 1 | tf_op jit(solution)/shard_map/pallas_call | solution.py:189
  28.8 1.2 collective-permute-start.4
  30.0 0.9 collective-permute-start.5
  31.1 10.3 %collective-permute-done.3.refs_5_ = bf16[2,64,2880]{2,1,0:T(8,128)(2,1)S(1)} collective-permute-done((bf16[2,64,2880]{2,1,0:T(8,128)(2,1)}, bf16[2,64,2880]{2,1,0:T(8,128)(2,1)S(1)}, u32[]{:S(2)}, u32[]{:S(2)}) %collective-permute-start.3) | collective-permute-done | bytes 737312 | tf_op jit(solution)/shard_map/ppermute | solution.py:24
  41.4 0.9 copy-done.5
  42.3 6.8 %shard_map.112.refs_0_ = f32[2,64,2880]{2,1,0:T(8,128)} custom-call(s32[1]{0:T(128)} %bitcast.ctx_ref, s32[8]{0:T(128)} %order_ref.5, bf16[2880,512]{1,0:T(8,128)(2,1)} %bitcast.41, bf16[128,640]{1,0:T(8,128)(2,1)} %get-tuple-element.77.refs_0_, bf16[128,640]{1,0:T(8,128)(2,1)} %copy-done.2, bf16[128,640]{1,0:T(8,128)(2,1)} %copy-done.3, ...), custom_call_target="tpu_custom_call" | custom-call | flops 1 | bytes 1 | tf_op jit(solution)/shard_map/pallas_call | solution.py:189
  49.1 1.4 copy-done
  50.5 2.6 %shard_map.114.refs_4_.refs_7_ = bf16[720,2880]{1,0:T(8,128)(2,1)S(1)} custom-call(bf16[720,2880]{1,0:T(8,128)(2,1)} %collective-permute-done.7.source_ref, f32[2,64,2880]{2,1,0:T(8,128)S(1)} %copy-done), custom_call_target="tpu_custom_call" | custom-call | flops 1 | bytes 1 | tf_op jit(solution)/shard_map/pallas_call | solution.py:111
  53.2 4.3 %shard_map.113.refs_3_ = bf16[1440,2880]{1,0:T(8,128)(2,1)S(1)} custom-call(bf16[1440,2880]{1,0:T(8,128)(2,1)} %collective-permute-done.6.source_ref, f32[2,64,2880]{2,1,0:T(8,128)S(1)} %copy-done.1), custom_call_target="tpu_custom_call" | custom-call | flops 1 | bytes 1 | tf_op jit(solution)/shard_map/pallas_call | solution.py:111
  57.5 1.7 shard_map.115
  59.3 1.6 collective-permute-start.11
  60.9 1.2 collective-permute-start.8
  62.1 0.9 collective-permute-start.9
  63.0 1.4 collective-permute-start.10
  64.4 8.2 %collective-permute-done.8.refs_0_.refs_1_ = bf16[64,2880]{1,0:T(8,128)(2,1)S(1)} collective-permute-done((bf16[64,2880]{1,0:T(8,128)(2,1)S(1)}, bf16[64,2880]{1,0:T(8,128)(2,1)S(1)}, u32[]{:S(2)}, u32[]{:S(2)}) %collective-permute-start.8) | collective-permute-done | bytes 368672 | tf_op jit(solution)/shard_map/ppermute | solution.py:24
  72.6 5.1 %collective-permute-done.9.refs_1_.refs_2_ = bf16[64,2880]{1,0:T(8,128)(2,1)S(1)} collective-permute-done((bf16[64,2880]{1,0:T(8,128)(2,1)S(1)}, bf16[64,2880]{1,0:T(8,128)(2,1)S(1)}, u32[]{:S(2)}, u32[]{:S(2)}) %collective-permute-start.9) | collective-permute-done | bytes 368672 | tf_op jit(solution)/shard_map/ppermute | solution.py:24
  77.7 1.6 collective-permute-done.10.refs_2_.refs_3_
  79.3 1.4 shard_map.116
  80.8 1.8 collective-permute-start.12
  82.6 0.8 collective-permute-start.13
  83.4 1.5 collective-permute-start.14
  84.9 1.2 collective-permute-start.15
  86.1 9.1 %shard_map.117 = (bf16[64,2880]{1,0:T(8,128)(2,1)S(1)}, bf16[64,2880]{1,0:T(8,128)(2,1)S(1)}, bf16[64,2880]{1,0:T(8,128)(2,1)S(1)}, bf16[64,2880]{1,0:T(8,128)(2,1)S(1)}) custom-call(bf16[64,2880]{1,0:T(8,128)(2,1)S(1)} %get-tuple-element.86.refs_0_, bf16[64,2880]{1,0:T(8,128)(2,1)S(1)} %collective-permute-done.8.refs_0_.refs_1_, ...), custom_call_target="tpu_custom_call" | custom-call | flops 1 | bytes 1 | tf_op jit(solution)/shard_map/pallas_call | solution.py:336
  95.2 3.9 %collective-permute-done.14.refs_1_.refs_2_ = bf16[64,2880]{1,0:T(8,128)(2,1)S(1)} collective-permute-done((bf16[64,2880]{1,0:T(8,128)(2,1)S(1)}, bf16[64,2880]{1,0:T(8,128)(2,1)S(1)}, u32[]{:S(2)}, u32[]{:S(2)}) %collective-permute-start.14) | collective-permute-done | bytes 368672 | tf_op jit(solution)/shard_map/ppermute | solution.py:24
  99.3 1.4 shard_map.118
  100.8 1.4 collective-permute-start.16
  102.2 1.4 collective-permute-start.17
  103.6 0.5 collective-permute-start.18
  104.2 1.5 collective-permute-start.19
  105.7 9.1 %shard_map.119 = (bf16[64,2880]{1,0:T(8,128)(2,1)S(1)}, bf16[64,2880]{1,0:T(8,128)(2,1)S(1)}, bf16[64,2880]{1,0:T(8,128)(2,1)S(1)}, bf16[64,2880]{1,0:T(8,128)(2,1)S(1)}) custom-call(bf16[64,2880]{1,0:T(8,128)(2,1)S(1)} %get-tuple-element.95.refs_8_.refs_0_, bf16[64,2880]{1,0:T(8,128)(2,1)S(1)} %collective-permute-done.13.refs_0_.refs_1_, ...), custom_call_target="tpu_custom_call" | custom-call | flops 1 | bytes 1 | tf_op jit(solution)/shard_map/pallas_call | solution.py:336
  114.7 1.5 collective-permute-start.23
  116.3 0.5 collective-permute-start.24
  116.8 1.5 collective-permute-start.25
  118.3 4.0 %collective-permute-done.19.refs_2_.refs_3_ = bf16[64,2880]{1,0:T(8,128)(2,1)S(1)} collective-permute-done((bf16[64,2880]{1,0:T(8,128)(2,1)S(1)}, bf16[64,2880]{1,0:T(8,128)(2,1)S(1)}, u32[]{:S(2)}, u32[]{:S(2)}) %collective-permute-start.19) | collective-permute-done | bytes 368672 | tf_op jit(solution)/shard_map/ppermute | solution.py:24
  122.3 1.4 shard_map.120
  124.2 1.0 collective-permute-start.21
  125.1 9.1 %shard_map.121 = (bf16[64,2880]{1,0:T(8,128)(2,1)S(1)}, bf16[64,2880]{1,0:T(8,128)(2,1)S(1)}, bf16[64,2880]{1,0:T(8,128)(2,1)S(1)}, bf16[64,2880]{1,0:T(8,128)(2,1)S(1)}) custom-call(bf16[64,2880]{1,0:T(8,128)(2,1)S(1)} %get-tuple-element.112.refs_8_.refs_0_, bf16[64,2880]{1,0:T(8,128)(2,1)S(1)} %collective-permute-done.17.refs_0_.refs_1_, ...), custom_call_target="tpu_custom_call" | custom-call | flops 1 | bytes 1 | tf_op jit(solution)/shard_map/pallas_call | solution.py:336
  134.2 1.9 collective-permute-done.24.refs_2_
  136.1 2.2 %collective-permute-done.25.refs_3_ = bf16[64,2880]{1,0:T(8,128)(2,1)S(1)} collective-permute-done((bf16[64,2880]{1,0:T(8,128)(2,1)S(1)}, bf16[64,2880]{1,0:T(8,128)(2,1)S(1)}, u32[]{:S(2)}, u32[]{:S(2)}) %collective-permute-start.25) | collective-permute-done | bytes 368672 | tf_op jit(solution)/shard_map/ppermute | solution.py:24
  138.7 0.9 collective-permute-start.35
  140.0 1.5 collective-permute-start.22
  141.6 3.6 %collective-permute-done.20.refs_1_ = bf16[64,2880]{1,0:T(8,128)(2,1)S(1)} collective-permute-done((bf16[64,2880]{1,0:T(8,128)(2,1)S(1)}, bf16[64,2880]{1,0:T(8,128)(2,1)S(1)}, u32[]{:S(2)}, u32[]{:S(2)}) %collective-permute-start.20) | collective-permute-done | bytes 368672 | tf_op jit(solution)/shard_map/ppermute | solution.py:24
  145.2 1.8 collective-permute-start.33
  147.0 0.8 collective-permute-start.34
  147.8 14.6 %collective-permute-done.22.refs_3_ = bf16[64,2880]{1,0:T(8,128)(2,1)S(1)} collective-permute-done((bf16[64,2880]{1,0:T(8,128)(2,1)S(1)}, bf16[64,2880]{1,0:T(8,128)(2,1)S(1)}, u32[]{:S(2)}, u32[]{:S(2)}) %collective-permute-start.22) | collective-permute-done | bytes 368672 | tf_op jit(solution)/shard_map/ppermute | solution.py:24
  162.4 7.6 %shard_map.123 = (bf16[64,2880]{1,0:T(8,128)(2,1)S(1)}, bf16[64,2880]{1,0:T(8,128)(2,1)S(1)}, bf16[64,2880]{1,0:T(8,128)(2,1)S(1)}, bf16[64,2880]{1,0:T(8,128)(2,1)S(1)}) custom-call(bf16[64,2880]{1,0:T(8,128)(2,1)S(1)} %get-tuple-element.118.refs_8_.refs_0_, bf16[64,2880]{1,0:T(8,128)(2,1)S(1)} %collective-permute-done.20.refs_1_, ...), custom_call_target="tpu_custom_call" | custom-call | flops 1 | bytes 1 | tf_op jit(solution)/shard_map/pallas_call | solution.py:336
  170.5 0.7 collective-permute-start.36
  172.0 2.6 %collective-permute-start.31 = (bf16[64,2880]{1,0:T(8,128)(2,1)S(1)}, bf16[64,2880]{1,0:T(8,128)(2,1)S(1)}, u32[]{:S(2)}, u32[]{:S(2)}) collective-permute-start(bf16[64,2880]{1,0:T(8,128)(2,1)S(1)} %get-tuple-element.133.refs_8_), channel_id=1, source_target_pairs={{0,24},{8,16},{16,8},{24,0},{1,25},{9,17},{17,9},{25,1},{2,26},{10... | collective-permute-start | bytes 1105928 | tf_op jit(solution)/shard_map/ppermute | solution.py:24
  174.6 4.1 %collective-permute-done.29.refs_1_ = bf16[64,2880]{1,0:T(8,128)(2,1)S(1)} collective-permute-done((bf16[64,2880]{1,0:T(8,128)(2,1)S(1)}, bf16[64,2880]{1,0:T(8,128)(2,1)S(1)}, u32[]{:S(2)}, u32[]{:S(2)}) %collective-permute-start.29) | collective-permute-done | bytes 368672 | tf_op jit(solution)/shard_map/ppermute | solution.py:24
  178.7 5.0 %collective-permute-done.30.refs_2_ = bf16[64,2880]{1,0:T(8,128)(2,1)S(1)} collective-permute-done((bf16[64,2880]{1,0:T(8,128)(2,1)S(1)}, bf16[64,2880]{1,0:T(8,128)(2,1)S(1)}, u32[]{:S(2)}, u32[]{:S(2)}) %collective-permute-start.30) | collective-permute-done | bytes 368672 | tf_op jit(solution)/shard_map/ppermute | solution.py:24
  183.7 1.4 collective-permute-done.31.refs_3_
  185.2 1.7 collective-permute-done.36.refs_4_
  187.3 2.3 %collective-permute-start.37 = (bf16[2,64,2880]{2,1,0:T(8,128)(2,1)S(1)}, bf16[2,64,2880]{2,1,0:T(8,128)(2,1)S(1)}, u32[]{:S(2)}, u32[]{:S(2)}) collective-permute-start(bf16[2,64,2880]{2,1,0:T(8,128)(2,1)S(1)} %shard_map.125.refs_5_), channel_id=1, source_target_pairs={{0,2},{1,3},{2,4},{3,5},{4,6},{5,7},{6,0},{7,1},{8,10},{9,11},{10,... | collective-permute-start | bytes 2211848 | tf_op jit(solution)/shard_map/ppermute | solution.py:31
  190.1 3.0 %collective-permute-start.28 = (bf16[64,2880]{1,0:T(8,128)(2,1)S(1)}, bf16[64,2880]{1,0:T(8,128)(2,1)S(1)}, u32[]{:S(2)}, u32[]{:S(2)}) collective-permute-start(bf16[64,2880]{1,0:T(8,128)(2,1)S(1)} %get-tuple-element.137), channel_id=1, source_target_pairs={{0,24},{8,16},{16,8},{24,0},{1,25},{9,17},{17,9},{25,1},{2,26},{10... | collective-permute-start | bytes 1105928 | tf_op jit(solution)/shard_map/ppermute | solution.py:24
  193.0 4.1 %collective-permute-done.26.refs_1_ = bf16[64,2880]{1,0:T(8,128)(2,1)S(1)} collective-permute-done((bf16[64,2880]{1,0:T(8,128)(2,1)S(1)}, bf16[64,2880]{1,0:T(8,128)(2,1)S(1)}, u32[]{:S(2)}, u32[]{:S(2)}) %collective-permute-start.26) | collective-permute-done | bytes 368672 | tf_op jit(solution)/shard_map/ppermute | solution.py:24
  197.1 4.0 %collective-permute-done.27.refs_2_ = bf16[64,2880]{1,0:T(8,128)(2,1)S(1)} collective-permute-done((bf16[64,2880]{1,0:T(8,128)(2,1)S(1)}, bf16[64,2880]{1,0:T(8,128)(2,1)S(1)}, u32[]{:S(2)}, u32[]{:S(2)}) %collective-permute-start.27) | collective-permute-done | bytes 368672 | tf_op jit(solution)/shard_map/ppermute | solution.py:24
  201.7 1.1 copy.16
  (69 shorter events, 5.2 us)
Async XLA Ops:
  2.1 8.2 %collective-permute-start = (bf16[128,640]{1,0:T(8,128)(2,1)}, bf16[128,640]{1,0:T(8,128)(2,1)S(1)}, u32[]{:S(2)}, u32[]{:S(2)}) collective-permute-start(bf16[128,640]{1,0:T(8,128)(2,1)} %get-tuple-element.74), channel_id=1, source_target_pairs={{0,8},{8,0},{16,24},{24,16},{1,9},{9,1},{17,25},{25,17},{2,10},{10... | collective-permute-start | bytes 491528 | tf_op jit(solution)/shard_map/ppermute | solution.py:24
  5.1 9.4 %collective-permute-start.1 = (bf16[128,640]{1,0:T(8,128)(2,1)}, bf16[128,640]{1,0:T(8,128)(2,1)S(1)}, u32[]{:S(2)}, u32[]{:S(2)}) collective-permute-start(bf16[128,640]{1,0:T(8,128)(2,1)} %get-tuple-element.75), channel_id=1, source_target_pairs={{0,16},{8,24},{16,0},{24,8},{1,17},{9,25},{17,1},{25,9},{2,18},{10... | collective-permute-start | bytes 491528 | tf_op jit(solution)/shard_map/ppermute | solution.py:24
  6.6 7.9 %collective-permute-start.2 = (bf16[128,640]{1,0:T(8,128)(2,1)}, bf16[128,640]{1,0:T(8,128)(2,1)S(1)}, u32[]{:S(2)}, u32[]{:S(2)}) collective-permute-start(bf16[128,640]{1,0:T(8,128)(2,1)} %get-tuple-element.76), channel_id=1, source_target_pairs={{0,24},{8,16},{16,8},{24,0},{1,25},{9,17},{17,9},{25,1},{2,26},{10... | collective-permute-start | bytes 491528 | tf_op jit(solution)/shard_map/ppermute | solution.py:24
  10.3 4.7 %copy-start.2 = (bf16[128,640]{1,0:T(8,128)(2,1)}, bf16[128,640]{1,0:T(8,128)(2,1)S(1)}, u32[]{:S(2)}) copy-start(bf16[128,640]{1,0:T(8,128)(2,1)S(1)} %collective-permute-done.refs_1_) | copy-start | bytes 491524
  14.5 0.7 copy-start.3
  14.5 0.7 copy-start.4
  14.5 38.7 %collective-permute-start.6 = (bf16[1440,2880]{1,0:T(8,128)(2,1)}, bf16[1440,2880]{1,0:T(8,128)(2,1)}, u32[]{:S(2)}, u32[]{:S(2)}) collective-permute-start(bf16[1440,2880]{1,0:T(8,128)(2,1)} %bitcast.24), channel_id=1, source_target_pairs={{0,1},{1,0},{2,3},{3,2},{4,5},{5,4},{6,7},{7,6},{8,9},{9,8},{10,11... | collective-permute-start | bytes 24883208 | tf_op jit(solution)/shard_map/ppermute | solution.py:36
  14.6 34.6 %collective-permute-start.7 = (bf16[720,2880]{1,0:T(8,128)(2,1)}, bf16[720,2880]{1,0:T(8,128)(2,1)}, u32[]{:S(2)}, u32[]{:S(2)}) collective-permute-start(bf16[720,2880]{1,0:T(8,128)(2,1)} %bitcast.31), channel_id=1, source_target_pairs={{0,1},{1,0},{2,3},{3,2},{4,5},{5,4},{6,7},{7,6},{8,9},{9,8},{10,11... | collective-permute-start | bytes 12441608 | tf_op jit(solution)/shard_map/ppermute | solution.py:36
  15.2 15.6 %copy-start.6 = (f32[2880]{0:T(1024)S(1)}, f32[2880]{0:T(1024)}, u32[]{:S(2)}) copy-start(f32[2880]{0:T(1024)} %param.16) | copy-start | bytes 34564
  15.2 15.6 %copy-start.7 = (f32[1,128,4]{1,2,0:T(4,128)S(1)}, f32[1,128,4]{1,2,0:T(4,128)}, u32[]{:S(2)}) copy-start(f32[1,128,4]{1,2,0:T(4,128)} %param.19) | copy-start | bytes 6148
  15.2 15.7 %copy-start.8 = (s32[1,128,4]{1,2,0:T(4,128)S(1)}, s32[1,128,4]{1,2,0:T(4,128)}, u32[]{:S(2)}) copy-start(s32[1,128,4]{1,2,0:T(4,128)} %param.18) | copy-start | bytes 6148
  20.5 20.9 %collective-permute-start.3 = (bf16[2,64,2880]{2,1,0:T(8,128)(2,1)}, bf16[2,64,2880]{2,1,0:T(8,128)(2,1)S(1)}, u32[]{:S(2)}, u32[]{:S(2)}) collective-permute-start(bf16[2,64,2880]{2,1,0:T(8,128)(2,1)} %shard_map.110.refs_4_), channel_id=1, source_target_pairs={{0,24},{8,16},{16,8},{24,0},{1,25},{9,17},{17,9},{25,1},{2,26},{10... | collective-permute-start | bytes 2211848 | tf_op jit(solution)/shard_map/ppermute | solution.py:24
  28.8 28.7 %collective-permute-start.4 = (bf16[2,64,2880]{2,1,0:T(8,128)(2,1)}, bf16[2,64,2880]{2,1,0:T(8,128)(2,1)S(1)}, u32[]{:S(2)}, u32[]{:S(2)}) collective-permute-start(bf16[2,64,2880]{2,1,0:T(8,128)(2,1)} %get-tuple-element.81.refs_6_), channel_id=1, source_target_pairs={{0,16},{8,24},{16,0},{24,8},{1,17},{9,25},{17,1},{25,9},{2,18},{10... | collective-permute-start | bytes 2211848 | tf_op jit(solution)/shard_map/ppermute | solution.py:24
  30.0 27.6 %collective-permute-start.5 = (bf16[2,64,2880]{2,1,0:T(8,128)(2,1)}, bf16[2,64,2880]{2,1,0:T(8,128)(2,1)S(1)}, u32[]{:S(2)}, u32[]{:S(2)}) collective-permute-start(bf16[2,64,2880]{2,1,0:T(8,128)(2,1)} %get-tuple-element.82), channel_id=1, source_target_pairs={{0,8},{8,0},{16,24},{24,16},{1,9},{9,1},{17,25},{25,17},{2,10},{10... | collective-permute-start | bytes 2211848 | tf_op jit(solution)/shard_map/ppermute | solution.py:24
  41.4 0.9 copy-start.5
  49.1 1.4 copy-start
  50.5 2.7 %copy-start.1 = (f32[2,64,2880]{2,1,0:T(8,128)S(1)}, f32[2,64,2880]{2,1,0:T(8,128)}, u32[]{:S(2)}) copy-start(f32[2,64,2880]{2,1,0:T(8,128)} %shard_map.112.refs_0_) | copy-start | bytes 4423684
  50.5 35.5 %slice-start.3 = ((s8[4239360]{0:T(1024)(128)(4,1)}), s8[4194304]{0:T(1024)(128)(4,1)S(1)}, s32[]{:S(2)}) async-start(s8[4239360]{0:T(1024)(128)(4,1)} %bitcast.32), calls=%async_computation.3 | async-start | bytes 8388608
  53.2 32.9 %slice-start.4 = ((s8[4239360]{0:T(1024)(128)(4,1)}), s8[45056]{0:T(1024)(128)(4,1)S(1)}, s32[]{:S(2)}) async-start(s8[4239360]{0:T(1024)(128)(4,1)} %bitcast.32), calls=%async_computation.4 | async-start | bytes 90112
  53.2 32.9 %slice-start = ((s8[8478720]{0:T(1024)(128)(4,1)}), s8[4194304]{0:T(1024)(128)(4,1)S(1)}, s32[]{:S(2)}) async-start(s8[8478720]{0:T(1024)(128)(4,1)} %bitcast.25), calls=%async_computation | async-start | bytes 8388608
  53.2 32.9 %slice-start.1 = ((s8[8478720]{0:T(1024)(128)(4,1)}), s8[4194304]{0:T(1024)(128)(4,1)S(1)}, s32[]{:S(2)}) async-start(s8[8478720]{0:T(1024)(128)(4,1)} %bitcast.25), calls=%async_computation.1 | async-start | bytes 8388608
  57.5 28.6 %slice-start.2 = ((s8[8478720]{0:T(1024)(128)(4,1)}), s8[90112]{0:T(1024)(128)(4,1)S(1)}, s32[]{:S(2)}) async-start(s8[8478720]{0:T(1024)(128)(4,1)} %bitcast.25), calls=%async_computation.2 | async-start | bytes 180224
  59.3 20.0 %collective-permute-start.11 = (bf16[2,64,2944]{2,1,0:T(8,128)(2,1)S(1)}, bf16[2,64,2944]{2,1,0:T(8,128)(2,1)S(1)}, u32[]{:S(2)}, u32[]{:S(2)}) collective-permute-start(bf16[2,64,2944]{2,1,0:T(8,128)(2,1)S(1)} %get-tuple-element.90), channel_id=1, source_target_pairs={{0,2},{1,3},{2,4},{3,5},{4,6},{5,7},{6,0},{7,1},{8,10},{9,11},{10,... | collective-permute-start | bytes 2261000 | tf_op jit(solution)/shard_map/ppermute | solution.py:31
  60.9 11.7 %collective-permute-start.8 = (bf16[64,2880]{1,0:T(8,128)(2,1)S(1)}, bf16[64,2880]{1,0:T(8,128)(2,1)S(1)}, u32[]{:S(2)}, u32[]{:S(2)}) collective-permute-start(bf16[64,2880]{1,0:T(8,128)(2,1)S(1)} %get-tuple-element.87), channel_id=1, source_target_pairs={{0,8},{8,0},{16,24},{24,16},{1,9},{9,1},{17,25},{25,17},{2,10},{10... | collective-permute-start | bytes 1105928 | tf_op jit(solution)/shard_map/ppermute | solution.py:24
  62.1 15.6 %collective-permute-start.9 = (bf16[64,2880]{1,0:T(8,128)(2,1)S(1)}, bf16[64,2880]{1,0:T(8,128)(2,1)S(1)}, u32[]{:S(2)}, u32[]{:S(2)}) collective-permute-start(bf16[64,2880]{1,0:T(8,128)(2,1)S(1)} %get-tuple-element.88), channel_id=1, source_target_pairs={{0,16},{8,24},{16,0},{24,8},{1,17},{9,25},{17,1},{25,9},{2,18},{10... | collective-permute-start | bytes 1105928 | tf_op jit(solution)/shard_map/ppermute | solution.py:24
  63.0 16.4 %collective-permute-start.10 = (bf16[64,2880]{1,0:T(8,128)(2,1)S(1)}, bf16[64,2880]{1,0:T(8,128)(2,1)S(1)}, u32[]{:S(2)}, u32[]{:S(2)}) collective-permute-start(bf16[64,2880]{1,0:T(8,128)(2,1)S(1)} %get-tuple-element.89), channel_id=1, source_target_pairs={{0,24},{8,16},{16,8},{24,0},{1,25},{9,17},{17,9},{25,1},{2,26},{10... | collective-permute-start | bytes 1105928 | tf_op jit(solution)/shard_map/ppermute | solution.py:24
  80.8 18.6 %collective-permute-start.12 = (bf16[2,64,2944]{2,1,0:T(8,128)(2,1)S(1)}, bf16[2,64,2944]{2,1,0:T(8,128)(2,1)S(1)}, u32[]{:S(2)}, u32[]{:S(2)}) collective-permute-start(bf16[2,64,2944]{2,1,0:T(8,128)(2,1)S(1)} %collective-permute-done.11.held_ref), channel_id=1, source_target_pairs={{0,2},{1,3},{2,4},{3,5},{4,6},{5,7},{6,0},{7,1},{8,10},{9,11},{10,... | collective-permute-start | bytes 2261000 | tf_op jit(solution)/shard_map/ppermute | solution.py:31
  82.6 12.6 %collective-permute-start.13 = (bf16[64,2880]{1,0:T(8,128)(2,1)S(1)}, bf16[64,2880]{1,0:T(8,128)(2,1)S(1)}, u32[]{:S(2)}, u32[]{:S(2)}) collective-permute-start(bf16[64,2880]{1,0:T(8,128)(2,1)S(1)} %get-tuple-element.101), channel_id=1, source_target_pairs={{0,8},{8,0},{16,24},{24,16},{1,9},{9,1},{17,25},{25,17},{2,10},{10... | collective-permute-start | bytes 1105928 | tf_op jit(solution)/shard_map/ppermute | solution.py:24
  83.4 15.8 %collective-permute-start.14 = (bf16[64,2880]{1,0:T(8,128)(2,1)S(1)}, bf16[64,2880]{1,0:T(8,128)(2,1)S(1)}, u32[]{:S(2)}, u32[]{:S(2)}) collective-permute-start(bf16[64,2880]{1,0:T(8,128)(2,1)S(1)} %get-tuple-element.102), channel_id=1, source_target_pairs={{0,16},{8,24},{16,0},{24,8},{1,17},{9,25},{17,1},{25,9},{2,18},{10... | collective-permute-start | bytes 1105928 | tf_op jit(solution)/shard_map/ppermute | solution.py:24
  84.9 14.2 %collective-permute-start.15 = (bf16[64,2880]{1,0:T(8,128)(2,1)S(1)}, bf16[64,2880]{1,0:T(8,128)(2,1)S(1)}, u32[]{:S(2)}, u32[]{:S(2)}) collective-permute-start(bf16[64,2880]{1,0:T(8,128)(2,1)S(1)} %get-tuple-element.103), channel_id=1, source_target_pairs={{0,24},{8,16},{16,8},{24,0},{1,25},{9,17},{17,9},{25,1},{2,26},{10... | collective-permute-start | bytes 1105928 | tf_op jit(solution)/shard_map/ppermute | solution.py:24
  100.8 21.5 %collective-permute-start.16 = (bf16[2,64,2944]{2,1,0:T(8,128)(2,1)S(1)}, bf16[2,64,2944]{2,1,0:T(8,128)(2,1)S(1)}, u32[]{:S(2)}, u32[]{:S(2)}) collective-permute-start(bf16[2,64,2944]{2,1,0:T(8,128)(2,1)S(1)} %collective-permute-done.12.held_ref), channel_id=1, source_target_pairs={{0,2},{1,3},{2,4},{3,5},{4,6},{5,7},{6,0},{7,1},{8,10},{9,11},{10,... | collective-permute-start | bytes 2261000 | tf_op jit(solution)/shard_map/ppermute | solution.py:31
  102.2 14.1 %collective-permute-start.17 = (bf16[64,2880]{1,0:T(8,128)(2,1)S(1)}, bf16[64,2880]{1,0:T(8,128)(2,1)S(1)}, u32[]{:S(2)}, u32[]{:S(2)}) collective-permute-start(bf16[64,2880]{1,0:T(8,128)(2,1)S(1)} %get-tuple-element.109), channel_id=1, source_target_pairs={{0,8},{8,0},{16,24},{24,16},{1,9},{9,1},{17,25},{25,17},{2,10},{10... | collective-permute-start | bytes 1105928 | tf_op jit(solution)/shard_map/ppermute | solution.py:24
  103.6 13.2 %collective-permute-start.18 = (bf16[64,2880]{1,0:T(8,128)(2,1)S(1)}, bf16[64,2880]{1,0:T(8,128)(2,1)S(1)}, u32[]{:S(2)}, u32[]{:S(2)}) collective-permute-start(bf16[64,2880]{1,0:T(8,128)(2,1)S(1)} %get-tuple-element.110), channel_id=1, source_target_pairs={{0,16},{8,24},{16,0},{24,8},{1,17},{9,25},{17,1},{25,9},{2,18},{10... | collective-permute-start | bytes 1105928 | tf_op jit(solution)/shard_map/ppermute | solution.py:24
  104.2 18.1 %collective-permute-start.19 = (bf16[64,2880]{1,0:T(8,128)(2,1)S(1)}, bf16[64,2880]{1,0:T(8,128)(2,1)S(1)}, u32[]{:S(2)}, u32[]{:S(2)}) collective-permute-start(bf16[64,2880]{1,0:T(8,128)(2,1)S(1)} %get-tuple-element.111), channel_id=1, source_target_pairs={{0,24},{8,16},{16,8},{24,0},{1,25},{9,17},{17,9},{25,1},{2,26},{10... | collective-permute-start | bytes 1105928 | tf_op jit(solution)/shard_map/ppermute | solution.py:24
  114.7 19.5 %collective-permute-start.23 = (bf16[64,2880]{1,0:T(8,128)(2,1)S(1)}, bf16[64,2880]{1,0:T(8,128)(2,1)S(1)}, u32[]{:S(2)}, u32[]{:S(2)}) collective-permute-start(bf16[64,2880]{1,0:T(8,128)(2,1)S(1)} %get-tuple-element.123), channel_id=1, source_target_pairs={{0,8},{8,0},{16,24},{24,16},{1,9},{9,1},{17,25},{25,17},{2,10},{10... | collective-permute-start | bytes 1105928 | tf_op jit(solution)/shard_map/ppermute | solution.py:24
  116.3 19.8 %collective-permute-start.24 = (bf16[64,2880]{1,0:T(8,128)(2,1)S(1)}, bf16[64,2880]{1,0:T(8,128)(2,1)S(1)}, u32[]{:S(2)}, u32[]{:S(2)}) collective-permute-start(bf16[64,2880]{1,0:T(8,128)(2,1)S(1)} %get-tuple-element.124), channel_id=1, source_target_pairs={{0,16},{8,24},{16,0},{24,8},{1,17},{9,25},{17,1},{25,9},{2,18},{10... | collective-permute-start | bytes 1105928 | tf_op jit(solution)/shard_map/ppermute | solution.py:24
  116.8 21.5 %collective-permute-start.25 = (bf16[64,2880]{1,0:T(8,128)(2,1)S(1)}, bf16[64,2880]{1,0:T(8,128)(2,1)S(1)}, u32[]{:S(2)}, u32[]{:S(2)}) collective-permute-start(bf16[64,2880]{1,0:T(8,128)(2,1)S(1)} %get-tuple-element.125), channel_id=1, source_target_pairs={{0,24},{8,16},{16,8},{24,0},{1,25},{9,17},{17,9},{25,1},{2,26},{10... | collective-permute-start | bytes 1105928 | tf_op jit(solution)/shard_map/ppermute | solution.py:24
  123.7 21.5 %collective-permute-start.20 = (bf16[64,2880]{1,0:T(8,128)(2,1)S(1)}, bf16[64,2880]{1,0:T(8,128)(2,1)S(1)}, u32[]{:S(2)}, u32[]{:S(2)}) collective-permute-start(bf16[64,2880]{1,0:T(8,128)(2,1)S(1)} %get-tuple-element.119), channel_id=1, source_target_pairs={{0,8},{8,0},{16,24},{24,16},{1,9},{9,1},{17,25},{25,17},{2,10},{10... | collective-permute-start | bytes 1105928 | tf_op jit(solution)/shard_map/ppermute | solution.py:24
  124.2 22.8 %collective-permute-start.21 = (bf16[64,2880]{1,0:T(8,128)(2,1)S(1)}, bf16[64,2880]{1,0:T(8,128)(2,1)S(1)}, u32[]{:S(2)}, u32[]{:S(2)}) collective-permute-start(bf16[64,2880]{1,0:T(8,128)(2,1)S(1)} %get-tuple-element.120), channel_id=1, source_target_pairs={{0,16},{8,24},{16,0},{24,8},{1,17},{9,25},{17,1},{25,9},{2,18},{10... | collective-permute-start | bytes 1105928 | tf_op jit(solution)/shard_map/ppermute | solution.py:24
  138.7 31.4 %collective-permute-start.35 = (bf16[2,64,2880]{2,1,0:T(8,128)(2,1)S(1)}, bf16[2,64,2880]{2,1,0:T(8,128)(2,1)S(1)}, u32[]{:S(2)}, u32[]{:S(2)}) collective-permute-start(bf16[2,64,2880]{2,1,0:T(8,128)(2,1)S(1)} %shard_map.122.refs_8_), channel_id=1, source_target_pairs={{0,2},{1,3},{2,4},{3,5},{4,6},{5,7},{6,0},{7,1},{8,10},{9,11},{10,... | collective-permute-start | bytes 2211848 | tf_op jit(solution)/shard_map/ppermute | solution.py:31
  139.6 30.4 %collective-permute-start.32 = (bf16[64,2880]{1,0:T(8,128)(2,1)S(1)}, bf16[64,2880]{1,0:T(8,128)(2,1)S(1)}, u32[]{:S(2)}, u32[]{:S(2)}) collective-permute-start(bf16[64,2880]{1,0:T(8,128)(2,1)S(1)} %get-tuple-element.127.refs_5_), channel_id=1, source_target_pairs={{0,8},{8,0},{16,24},{24,16},{1,9},{9,1},{17,25},{25,17},{2,10},{10... | collective-permute-start | bytes 1105928 | tf_op jit(solution)/shard_map/ppermute | solution.py:24
  140.0 22.4 %collective-permute-start.22 = (bf16[64,2880]{1,0:T(8,128)(2,1)S(1)}, bf16[64,2880]{1,0:T(8,128)(2,1)S(1)}, u32[]{:S(2)}, u32[]{:S(2)}) collective-permute-start(bf16[64,2880]{1,0:T(8,128)(2,1)S(1)} %get-tuple-element.121), channel_id=1, source_target_pairs={{0,24},{8,16},{16,8},{24,0},{1,25},{9,17},{17,9},{25,1},{2,26},{10... | collective-permute-start | bytes 1105928 | tf_op jit(solution)/shard_map/ppermute | solution.py:24
  145.2 24.8 %collective-permute-start.33 = (bf16[64,2880]{1,0:T(8,128)(2,1)S(1)}, bf16[64,2880]{1,0:T(8,128)(2,1)S(1)}, u32[]{:S(2)}, u32[]{:S(2)}) collective-permute-start(bf16[64,2880]{1,0:T(8,128)(2,1)S(1)} %get-tuple-element.128.refs_6_), channel_id=1, source_target_pairs={{0,16},{8,24},{16,0},{24,8},{1,17},{9,25},{17,1},{25,9},{2,18},{10... | collective-permute-start | bytes 1105928 | tf_op jit(solution)/shard_map/ppermute | solution.py:24
  147.0 23.1 %collective-permute-start.34 = (bf16[64,2880]{1,0:T(8,128)(2,1)S(1)}, bf16[64,2880]{1,0:T(8,128)(2,1)S(1)}, u32[]{:S(2)}, u32[]{:S(2)}) collective-permute-start(bf16[64,2880]{1,0:T(8,128)(2,1)S(1)} %get-tuple-element.129.refs_7_), channel_id=1, source_target_pairs={{0,24},{8,16},{16,8},{24,0},{1,25},{9,17},{17,9},{25,1},{2,26},{10... | collective-permute-start | bytes 1105928 | tf_op jit(solution)/shard_map/ppermute | solution.py:24
  170.5 16.4 %collective-permute-start.36 = (bf16[2,64,2880]{2,1,0:T(8,128)(2,1)S(1)}, bf16[2,64,2880]{2,1,0:T(8,128)(2,1)S(1)}, u32[]{:S(2)}, u32[]{:S(2)}) collective-permute-start(bf16[2,64,2880]{2,1,0:T(8,128)(2,1)S(1)} %shard_map.124.refs_5_), channel_id=1, source_target_pairs={{0,2},{1,3},{2,4},{3,5},{4,6},{5,7},{6,0},{7,1},{8,10},{9,11},{10,... | collective-permute-start | bytes 2211848 | tf_op jit(solution)/shard_map/ppermute | solution.py:31
  171.1 7.6 %collective-permute-start.29 = (bf16[64,2880]{1,0:T(8,128)(2,1)S(1)}, bf16[64,2880]{1,0:T(8,128)(2,1)S(1)}, u32[]{:S(2)}, u32[]{:S(2)}) collective-permute-start(bf16[64,2880]{1,0:T(8,128)(2,1)S(1)} %get-tuple-element.131.refs_6_), channel_id=1, source_target_pairs={{0,8},{8,0},{16,24},{24,16},{1,9},{9,1},{17,25},{25,17},{2,10},{10... | collective-permute-start | bytes 1105928 | tf_op jit(solution)/shard_map/ppermute | solution.py:24
  171.5 12.2 %collective-permute-start.30 = (bf16[64,2880]{1,0:T(8,128)(2,1)S(1)}, bf16[64,2880]{1,0:T(8,128)(2,1)S(1)}, u32[]{:S(2)}, u32[]{:S(2)}) collective-permute-start(bf16[64,2880]{1,0:T(8,128)(2,1)S(1)} %get-tuple-element.132.refs_7_), channel_id=1, source_target_pairs={{0,16},{8,24},{16,0},{24,8},{1,17},{9,25},{17,1},{25,9},{2,18},{10... | collective-permute-start | bytes 1105928 | tf_op jit(solution)/shard_map/ppermute | solution.py:24
  172.0 13.1 %collective-permute-start.31 = (bf16[64,2880]{1,0:T(8,128)(2,1)S(1)}, bf16[64,2880]{1,0:T(8,128)(2,1)S(1)}, u32[]{:S(2)}, u32[]{:S(2)}) collective-permute-start(bf16[64,2880]{1,0:T(8,128)(2,1)S(1)} %get-tuple-element.133.refs_8_), channel_id=1, source_target_pairs={{0,24},{8,16},{16,8},{24,0},{1,25},{9,17},{17,9},{25,1},{2,26},{10... | collective-permute-start | bytes 1105928 | tf_op jit(solution)/shard_map/ppermute | solution.py:24
  187.3 14.3 %collective-permute-start.37 = (bf16[2,64,2880]{2,1,0:T(8,128)(2,1)S(1)}, bf16[2,64,2880]{2,1,0:T(8,128)(2,1)S(1)}, u32[]{:S(2)}, u32[]{:S(2)}) collective-permute-start(bf16[2,64,2880]{2,1,0:T(8,128)(2,1)S(1)} %shard_map.125.refs_5_), channel_id=1, source_target_pairs={{0,2},{1,3},{2,4},{3,5},{4,6},{5,7},{6,0},{7,1},{8,10},{9,11},{10,... | collective-permute-start | bytes 2211848 | tf_op jit(solution)/shard_map/ppermute | solution.py:31
  189.5 7.6 %collective-permute-start.26 = (bf16[64,2880]{1,0:T(8,128)(2,1)S(1)}, bf16[64,2880]{1,0:T(8,128)(2,1)S(1)}, u32[]{:S(2)}, u32[]{:S(2)}) collective-permute-start(bf16[64,2880]{1,0:T(8,128)(2,1)S(1)} %get-tuple-element.135), channel_id=1, source_target_pairs={{0,8},{8,0},{16,24},{24,16},{1,9},{9,1},{17,25},{25,17},{2,10},{10... | collective-permute-start | bytes 1105928 | tf_op jit(solution)/shard_map/ppermute | solution.py:24
  189.5 11.6 %collective-permute-start.27 = (bf16[64,2880]{1,0:T(8,128)(2,1)S(1)}, bf16[64,2880]{1,0:T(8,128)(2,1)S(1)}, u32[]{:S(2)}, u32[]{:S(2)}) collective-permute-start(bf16[64,2880]{1,0:T(8,128)(2,1)S(1)} %get-tuple-element.136), channel_id=1, source_target_pairs={{0,16},{8,24},{16,0},{24,8},{1,17},{9,25},{17,1},{25,9},{2,18},{10... | collective-permute-start | bytes 1105928 | tf_op jit(solution)/shard_map/ppermute | solution.py:24
  190.1 11.1 %collective-permute-start.28 = (bf16[64,2880]{1,0:T(8,128)(2,1)S(1)}, bf16[64,2880]{1,0:T(8,128)(2,1)S(1)}, u32[]{:S(2)}, u32[]{:S(2)}) collective-permute-start(bf16[64,2880]{1,0:T(8,128)(2,1)S(1)} %get-tuple-element.137), channel_id=1, source_target_pairs={{0,24},{8,16},{16,8},{24,0},{1,25},{9,17},{17,9},{25,1},{2,26},{10... | collective-permute-start | bytes 1105928 | tf_op jit(solution)/shard_map/ppermute | solution.py:24

commit v2 on v1

--- a/solution.py
+++ b/solution.py
@@ -204,33 +204,61 @@
     )(ctx_scalar, order, weight, *got, *added, *after)
 
 
-def pick_and_mix(ctx_count, capacity, ctx_ref, plane_ref, held, route, out_refs, mix_ref):
-    tokens = held.shape[0]
-    count = ctx_count * capacity
-    lane = lax.broadcasted_iota(jnp.int32, (1, count), 1)
-    partner = ctx_ref[0] ^ (lane // capacity)
-    wanted = (partner * plane_ref[1] + plane_ref[0]).astype(jnp.float32)
-    member = jnp.zeros((tokens, count), jnp.float32)
-    weight = jnp.zeros((tokens, count), jnp.float32)
-    for k in range(TOPK):
-        chosen = route[:, k : k + 1] == wanted
-        member = jnp.where(chosen, 1.0, member)
-        weight = jnp.where(chosen, route[:, TOPK + k : TOPK + k + 1], weight)
-    row = lax.broadcasted_iota(jnp.int32, (tokens, tokens), 0)
-    earlier = lax.broadcasted_iota(jnp.int32, (tokens, tokens), 1) < row
-    rank = nn_dot(earlier.astype(jnp.bfloat16), member.astype(jnp.bfloat16))
-    slot = (lane % capacity).astype(jnp.float32)
-    placed = jnp.where(rank == slot, member, 0.0)
-    mix_ref[...] = (placed * weight).astype(jnp.bfloat16)
-    picked = nn_dot(placed.T.astype(jnp.bfloat16), held).astype(jnp.bfloat16)
+def mask_kernel(offsets, ctx_ref, plane_ref, *refs):
+    sources, outs = refs[: len(offsets)], refs[-2 * len(offsets) :]
+    for i, offset in enumerate(offsets):
+        mix_ref, place_ref = outs[2 * i : 2 * i + 2]
+        tokens, count = mix_ref.shape
+        capacity = plane_ref[2]
+        if len(sources[i].shape) == 3:
+            route = merged(sources[i][:, :, D - D % 128 :]).astype(jnp.float32)
+            offset = offset + D % 128
+        else:
+            route = sources[i][...].astype(jnp.float32)
+        lane = lax.broadcasted_iota(jnp.int32, (1, count), 1)
+        partner = ctx_ref[0] ^ (lane // capacity)
+        wanted = (partner * plane_ref[1] + plane_ref[0]).astype(jnp.float32)
+        member = jnp.zeros((tokens, count), jnp.float32)
+        weight = jnp.zeros((tokens, count), jnp.float32)
+        for k in range(offset, offset + TOPK):
+            chosen = route[:, k : k + 1] == wanted
+            member = jnp.where(chosen, 1.0, member)
+            weight = jnp.where(chosen, route[:, TOPK + k : TOPK + k + 1], weight)
+        row = lax.broadcasted_iota(jnp.int32, (tokens, tokens), 0)
+        earlier = lax.broadcasted_iota(jnp.int32, (tokens, tokens), 1) < row
+        rank = nn_dot(earlier.astype(jnp.bfloat16), member.astype(jnp.bfloat16))
+        slot = (lane % capacity).astype(jnp.float32)
+        placed = jnp.where(rank == slot, member, 0.0)
+        mix_ref[...] = (placed * weight).astype(jnp.bfloat16)
+        place_ref[...] = placed.T.astype(jnp.bfloat16)
+
+
+def masks(ctx_scalar, plane_scalars, sources, offsets, tokens, count):
+    shapes = [
+        jax.ShapeDtypeStruct((tokens, count), jnp.bfloat16),
+        jax.ShapeDtypeStruct((count, tokens), jnp.bfloat16),
+    ]
+    return pl.pallas_call(
+        functools.partial(mask_kernel, offsets),
+        out_shape=shapes * len(offsets),
+        in_specs=[SMEM_SPEC] * 2 + [VMEM_SPEC] * len(offsets),
+        out_specs=[VMEM_SPEC] * (2 * len(offsets)),
+        compiler_params=pltpu.CompilerParams(vmem_limit_bytes=6 << 20),
+        cost_estimate=SMALL_COST,
+    )(ctx_scalar, plane_scalars, *sources)
+
+
+def put_slots(place_ref, held, out_refs):
+    capacity = out_refs[0].shape[0]
+    picked = nn_dot(place_ref[...], held).astype(jnp.bfloat16)
     for d, out_ref in enumerate(out_refs):
         out_ref[...] = picked[d * capacity : (d + 1) * capacity]
 
 
-def norm_kernel(ctx_count, part_count, ctx_ref, plane_ref, gain_ref, route_ref, *refs):
+def norm_kernel(ctx_count, part_count, gain_ref, place_ref, route_ref, next_ref, *refs):
     part_refs = refs[:part_count]
-    residual_ref, normed_ref, mix_ref, *out_refs = refs[-3 - ctx_count :]
-    capacity, columns = out_refs[0].shape
+    residual_ref, normed_ref, *out_refs = refs[-2 - ctx_count :]
+    columns = residual_ref.shape[2]
     total = merged(part_refs[0][...])
     for part_ref in part_refs[1:]:
         total = total + merged(part_ref[...]).astype(jnp.float32)
@@ -239,62 +267,44 @@
     res_float = residual.astype(jnp.float32)
     mean = jnp.mean(res_float * res_float, axis=-1, keepdims=True)
     normed = (res_float * lax.rsqrt(mean + 1e-05) * gain_ref[...]).astype(jnp.bfloat16)
-    route = route_ref[...]
+    put_slots(place_ref, normed, out_refs)
+    route = route_ref[...] + next_ref[...]
     normed_ref[:, :, :columns] = normed.reshape(residual_ref.shape)
     normed_ref[:, :, columns:] = route.reshape(normed_ref.shape[:2] + route.shape[1:])
-    pick_and_mix(
-        ctx_count,
-        capacity,
-        ctx_ref,
-        plane_ref,
-        normed,
-        route.astype(jnp.float32),
-        out_refs,
-        mix_ref,
-    )
-
-
-def pick_shapes(ctx_count, capacity, tokens, columns):
-    slot = jax.ShapeDtypeStruct((capacity, columns), jnp.bfloat16)
-    return [jax.ShapeDtypeStruct((tokens, ctx_count * capacity), jnp.bfloat16)] + [slot] * ctx_count
-
-
-def norm_and_pick(ctx_scalar, plane_scalars, gain, route, parts, ctx_count, capacity, after):
+
+
+def norm_and_pick(gain, place, route, following, parts, ctx_count, after):
     _, half, columns = parts[0].shape
-    tokens, extra = route.shape
+    slot = jax.ShapeDtypeStruct((place.shape[0] // ctx_count, columns), jnp.bfloat16)
     return pl.pallas_call(
         functools.partial(norm_kernel, ctx_count, len(parts)),
         out_shape=[
             jax.ShapeDtypeStruct((2, half, columns), jnp.bfloat16),
-            jax.ShapeDtypeStruct((2, half, columns + extra), jnp.bfloat16),
+            jax.ShapeDtypeStruct((2, half, columns + route.shape[1]), jnp.bfloat16),
         ]
-        + pick_shapes(ctx_count, capacity, tokens, columns),
-        in_specs=[SMEM_SPEC] * 2 + [VMEM_SPEC] * (2 + len(parts)) + [ANY_SPEC] * len(after),
-        out_specs=[VMEM_SPEC] * (3 + ctx_count),
+        + [slot] * ctx_count,
+        in_specs=[VMEM_SPEC] * (4 + len(parts)) + [ANY_SPEC] * len(after),
+        out_specs=[VMEM_SPEC] * (2 + ctx_count),
         compiler_params=pltpu.CompilerParams(vmem_limit_bytes=12 << 20),
         cost_estimate=SMALL_COST,
-    )(ctx_scalar, plane_scalars, gain, route, *parts, *after)
-
-
-def pick_kernel(ctx_count, ctx_ref, plane_ref, held_ref, *refs):
-    mix_ref, *out_refs = refs[-1 - ctx_count :]
-    capacity, columns = out_refs[0].shape
-    held = merged(held_ref[:, :, :columns])
-    route = merged(held_ref[:, :, columns:]).astype(jnp.float32)
-    pick_and_mix(ctx_count, capacity, ctx_ref, plane_ref, held, route, out_refs, mix_ref)
-
-
-def pick_rows(ctx_scalar, plane_scalars, held, like, after):
+    )(gain, place, route, following, *parts, *after)
+
+
+def pick_kernel(ctx_count, place_ref, held_ref, *refs):
+    out_refs = refs[-ctx_count:]
+    put_slots(place_ref, merged(held_ref[:, :, : out_refs[0].shape[1]]), out_refs)
+
+
+def pick_rows(place, held, like, after):
     ctx_count = len(like)
-    capacity, columns = like[0].shape
     return pl.pallas_call(
         functools.partial(pick_kernel, ctx_count),
-        out_shape=pick_shapes(ctx_count, capacity, 2 * held.shape[1], columns),
-        in_specs=[SMEM_SPEC] * 2 + [VMEM_SPEC] + [ANY_SPEC] * len(after),
-        out_specs=[VMEM_SPEC] * (1 + ctx_count),
+        out_shape=[jax.ShapeDtypeStruct(like[0].shape, like[0].dtype)] * ctx_count,
+        in_specs=[VMEM_SPEC] * 2 + [ANY_SPEC] * len(after),
+        out_specs=[VMEM_SPEC] * ctx_count,
         compiler_params=pltpu.CompilerParams(vmem_limit_bytes=6 << 20),
         cost_estimate=SMALL_COST,
-    )(ctx_scalar, plane_scalars, held, *after)
+    )(place, held, *after)
 
 
 def expert_kernel(ctx_count, tile, *refs):
@@ -403,11 +413,21 @@
     planes = lax.axis_size("exp") // 2
     ctx_scalar = lax.axis_index("ctx").astype(jnp.int32).reshape(1)
     plane_index = (lax.axis_index("exp") // 2).astype(jnp.int32)
-    plane_scalars = jnp.stack([plane_index, jnp.full_like(plane_index, planes)])
     token_count = queries.shape[1]
     experts = ctx_count * planes
     capacity = 2 * token_count * TOPK // experts
     last = ctx_count - 1
+    plane_scalars = jnp.stack(
+        [plane_index, jnp.full_like(plane_index, planes), jnp.full_like(plane_index, capacity)]
+    )
+
+    route = jnp.concatenate(
+        [expert_ids[0].astype(jnp.bfloat16), route_weights[0].astype(jnp.bfloat16)], axis=1
+    )
+    spare = -D % 128
+    following = jnp.pad(route, ((0, 0), (2 * TOPK, spare - 4 * TOPK)))
+    route = jnp.pad(route, ((0, 0), (0, spare - 2 * TOPK)))
+    mask_shape = (token_count, ctx_count * capacity)
 
     packed = pack(ctx_scalar, queries[0], key_rows[0], value_matrix[0], ctx_count)
     got = [ctx_swap(packed[d], d) for d in range(ctx_count)]
@@ -426,23 +446,17 @@
     added = [hidden_columns, ctx_swap(first[0], last)]
     own = attend((0,), ctx_scalar, block_order, weight, got, added, parts[:1])
     parts = [ctx_swap(part, partners[i]) for i, part in enumerate(parts)]
+    following, _ = lax.optimization_barrier((following, added[1]))
+    following = plane_shift(following, 1)
+    mix, place, next_mix, next_place = masks(
+        ctx_scalar, plane_scalars, [route, following], (0, 2 * TOPK), *mask_shape
+    )
     other = [copy_after(w, list(own)) for w in swapped]
     gate_ups = [w.reshape(2, half, D) for w in (gate_up_mine, other[0])]
     downs = [down_mine, other[1]]
 
-    route = jnp.concatenate(
-        [expert_ids[0].astype(jnp.bfloat16), route_weights[0].astype(jnp.bfloat16)], axis=1
-    )
-    route = jnp.pad(route, ((0, 0), (0, -D % 128 - 2 * TOPK)))
-    residual, held, mix, *rows = norm_and_pick(
-        ctx_scalar,
-        plane_scalars,
-        norm_gain[None],
-        route,
-        list(own) + parts,
-        ctx_count,
-        capacity,
-        other,
+    residual, held, *rows = norm_and_pick(
+        norm_gain[None], place, route, following, list(own) + parts, ctx_count, other
     )
 
     def spread(blocks):
@@ -465,11 +479,17 @@
     done, carried = [], []
     for s in range(1, planes):
         held = plane_shift(held, 1)
-        mix, *rows = pick_rows(ctx_scalar, plane_scalars, held, rows, arrived[s - 1][1:] + done[:1])
+        mixes.append(next_mix)
+        rows = pick_rows(next_place, held, rows, arrived[s - 1][1:] + done[:1])
         held, rows = lax.optimization_barrier((held, rows))
-        mixes.append(mix)
         arrived.append(spread(rows))
-        done = run_expert(s - 1, list(rows[:1]))
+        after = list(rows[:1])
+        if s < planes - 1:
+            next_mix, next_place = masks(
+                ctx_scalar, plane_scalars, [held], (2 * TOPK,), *mask_shape
+            )
+            after.append(next_mix)
+        done = run_expert(s - 1, after)
         if s == 1:
             own_result = done
         if s > 2:

time: 203 us -> 199 us (0.980)
  waiting for transfers between devices: 83.9 us -> 78.9 us
    ppermute x30, waiting for transfers between devices: 82 us -> 77.9 us  [ctx_swap(): return lax.ppermute(rows, 'ctx', [(i, i ^ distance) for i in range(count)])]
    ppermute x30, starting transfers between devices: 35.1 us -> 37.4 us  [ctx_swap(): return lax.ppermute(rows, 'ctx', [(i, i ^ distance) for i in range(count)])]
    ppermute x6 -> x7, starting transfers between devices: 8.68 us -> 8.04 us  [plane_shift(): lax.ppermute(rows, 'exp', [(i, (i + 2 * planes) % count) for i in range(c...]
    pallas_call x3 -> x6, Pallas kernels: 4.31 us -> 4.89 us  [the longest x3 3.25 us: masks(): pl.pallas_call(functools.partial(mask_kernel, offsets), out_shape=shapes...]
  transfers between devices with their start and end apart: 38 -> 39, of which waited for: 19 -> 18; matrix products, arithmetic and copies ran while one was open for 0% -> 0% of each run, Pallas kernels for 31% -> 33%
where the time goes in v2:
time: 199 us; the launch traced here: 198 us
  waiting for transfers between devices  78.9 us (40%)
  Pallas kernels  69.9 us (35%)
  starting transfers between devices  46 us (23%)
  local copies, waits for them, and re-layouts  2.98 us (1%)
    ppermute x30, waiting for transfers between devices, ctx_swap(): return lax.ppermute(rows, 'ctx', [(i, i ^ distance) for i in range(count)])  77.9 us
    ppermute x30, starting transfers between devices, ctx_swap(): return lax.ppermute(rows, 'ctx', [(i, i ^ distance) for i in range(count)])  37.4 us
    pallas_call x4, Pallas kernels, expert(): pl.pallas_call(functools.partial(expert_kernel, ctx_count, tile), out_sha...  34.9 us
    pallas_call x3, Pallas kernels, attend(): pl.pallas_call(functools.partial(attend_kernel, dests, ctx_count), out_sh...  18.8 us
    ppermute x7, starting transfers between devices, plane_shift(): lax.ppermute(rows, 'exp', [(i, (i + 2 * planes) % count) for i in range(c...  8.04 us
    pallas_call x2, Pallas kernels, copy_after(): pl.pallas_call(copy_kernel, out_shape=jax.ShapeDtypeStruct(source.shape,...  6.58 us
  transfers between devices with their start and end apart: 39, of which 18 were waited for; matrix products, arithmetic and copies ran while one was open for 0% of the time, Pallas kernels for 33%

profile of v2, /device:TPU:0, one launch (start us, length us, event | category | flops | bytes accessed | tf_op | source)
XLA Modules:
  0.0 198.3 jit_solution(6166164466005605586)
XLA Ops:
  0.0 2.1 %shard_map.109 = (bf16[128,640]{1,0:T(8,128)(2,1)}, bf16[128,640]{1,0:T(8,128)(2,1)}, bf16[128,640]{1,0:T(8,128)(2,1)}, bf16[128,640]{1,0:T(8,128)(2,1)}) custom-call(s32[1]{0:T(128)} %bitcast.ctx_ref, bf16[128,2048]{1,0:T(8,128)(2,1)} %bitcast.43, bf16[128,256]{1,0:T(8,128)(2,1)} %bitcast.44, bf16[128,256]{1,0:T(8,128)(2,1)} %bitcast.45), custom_call_target="tpu_custom_call" | custom-call | flops 1 | bytes 1 | tf_op jit(solution)/shard_map/pallas_call | solution.py:94
  2.1 3.0 %collective-permute-start = (bf16[128,640]{1,0:T(8,128)(2,1)}, bf16[128,640]{1,0:T(8,128)(2,1)S(1)}, u32[]{:S(2)}, u32[]{:S(2)}) collective-permute-start(bf16[128,640]{1,0:T(8,128)(2,1)} %get-tuple-element.79), channel_id=1, source_target_pairs={{0,8},{8,0},{16,24},{24,16},{1,9},{9,1},{17,25},{25,17},{2,10},{10... | collective-permute-start | bytes 491528 | tf_op jit(solution)/shard_map/ppermute | solution.py:24
  5.1 1.5 collective-permute-start.1
  6.6 3.7 %collective-permute-done.refs_1_ = bf16[128,640]{1,0:T(8,128)(2,1)S(1)} collective-permute-done((bf16[128,640]{1,0:T(8,128)(2,1)}, bf16[128,640]{1,0:T(8,128)(2,1)S(1)}, u32[]{:S(2)}, u32[]{:S(2)}) %collective-permute-start) | collective-permute-done | bytes 163872 | tf_op jit(solution)/shard_map/ppermute | solution.py:24
  10.3 4.1 %collective-permute-done.1.refs_2_ = bf16[128,640]{1,0:T(8,128)(2,1)S(1)} collective-permute-done((bf16[128,640]{1,0:T(8,128)(2,1)}, bf16[128,640]{1,0:T(8,128)(2,1)S(1)}, u32[]{:S(2)}, u32[]{:S(2)}) %collective-permute-start.1) | collective-permute-done | bytes 163872 | tf_op jit(solution)/shard_map/ppermute | solution.py:24
  15.2 5.2 %shard_map.110.refs_4_ = bf16[2,64,2880]{2,1,0:T(8,128)(2,1)} custom-call(s32[1]{0:T(128)} %bitcast.ctx_ref, s32[8]{0:T(128)} %order_ref.5, bf16[2880,512]{1,0:T(8,128)(2,1)} %bitcast.39, bf16[128,640]{1,0:T(8,128)(2,1)} %get-tuple-element.82.refs_0_, bf16[128,640]{1,0:T(8,128)(2,1)} %copy-done.2, bf16[128,640]{1,0:T(8,128)(2,1)} %copy-done.3, ...), custom_call_target="tpu_custom_call" | custom-call | flops 1 | bytes 1 | tf_op jit(solution)/shard_map/pallas_call | solution.py:189
  20.4 1.6 collective-permute-start.3
  22.0 6.7 %shard_map.112 = (bf16[2,64,2880]{2,1,0:T(8,128)(2,1)}, bf16[2,64,2880]{2,1,0:T(8,128)(2,1)}) custom-call(s32[1]{0:T(128)} %bitcast.ctx_ref, s32[8]{0:T(128)} %order_ref.5, bf16[2880,512]{1,0:T(8,128)(2,1)} %bitcast.40, bf16[128,640]{1,0:T(8,128)(2,1)} %get-tuple-element.82.refs_0_, bf16[128,640]{1,0:T(8,128)(2,1)} %copy-done.2, bf16[128,640]{1,0:T(8,128)(2,1)} %copy-done.3, ...), custom_call_target="tpu_custom_call" | custom-call | flops 1 | bytes 1 | tf_op jit(solution)/shard_map/pallas_call | solution.py:189
  28.7 1.2 collective-permute-start.5
  30.0 0.8 collective-permute-start.6
  31.1 10.3 %collective-permute-done.3.refs_5_ = bf16[2,64,2880]{2,1,0:T(8,128)(2,1)S(1)} collective-permute-done((bf16[2,64,2880]{2,1,0:T(8,128)(2,1)}, bf16[2,64,2880]{2,1,0:T(8,128)(2,1)S(1)}, u32[]{:S(2)}, u32[]{:S(2)}) %collective-permute-start.3) | collective-permute-done | bytes 737312 | tf_op jit(solution)/shard_map/ppermute | solution.py:24
  41.4 1.6 collective-permute-start.4
  43.1 6.8 %shard_map.113.refs_0_ = f32[2,64,2880]{2,1,0:T(8,128)} custom-call(s32[1]{0:T(128)} %bitcast.ctx_ref, s32[8]{0:T(128)} %order_ref.5, bf16[2880,512]{1,0:T(8,128)(2,1)} %bitcast.41, bf16[128,640]{1,0:T(8,128)(2,1)} %get-tuple-element.82.refs_0_, bf16[128,640]{1,0:T(8,128)(2,1)} %copy-done.2, bf16[128,640]{1,0:T(8,128)(2,1)} %copy-done.3, ...), custom_call_target="tpu_custom_call" | custom-call | flops 1 | bytes 1 | tf_op jit(solution)/shard_map/pallas_call | solution.py:189
  49.9 1.2 shard_map.111
  51.2 1.4 copy-done
  52.5 2.6 %shard_map.115.refs_4_.refs_7_ = bf16[720,2880]{1,0:T(8,128)(2,1)S(1)} custom-call(bf16[720,2880]{1,0:T(8,128)(2,1)} %collective-permute-done.8.source_ref, f32[2,64,2880]{2,1,0:T(8,128)S(1)} %copy-done), custom_call_target="tpu_custom_call" | custom-call | flops 1 | bytes 1 | tf_op jit(solution)/shard_map/pallas_call | solution.py:111
  55.2 4.0 %shard_map.114.refs_3_ = bf16[1440,2880]{1,0:T(8,128)(2,1)S(1)} custom-call(bf16[1440,2880]{1,0:T(8,128)(2,1)} %collective-permute-done.7.source_ref, f32[2,64,2880]{2,1,0:T(8,128)S(1)} %copy-done.1), custom_call_target="tpu_custom_call" | custom-call | flops 1 | bytes 1 | tf_op jit(solution)/shard_map/pallas_call | solution.py:111
  59.2 1.0 shard_map.116
  60.2 1.6 collective-permute-start.12
  61.9 1.2 collective-permute-start.9
  63.0 0.9 collective-permute-start.10
  63.9 1.4 collective-permute-start.11
  65.3 8.2 %collective-permute-done.9.refs_0_.refs_1_ = bf16[64,2880]{1,0:T(8,128)(2,1)S(1)} collective-permute-done((bf16[64,2880]{1,0:T(8,128)(2,1)S(1)}, bf16[64,2880]{1,0:T(8,128)(2,1)S(1)}, u32[]{:S(2)}, u32[]{:S(2)}) %collective-permute-start.9) | collective-permute-done | bytes 368672 | tf_op jit(solution)/shard_map/ppermute | solution.py:24
  73.6 3.9 %collective-permute-done.10.refs_1_.refs_2_ = bf16[64,2880]{1,0:T(8,128)(2,1)S(1)} collective-permute-done((bf16[64,2880]{1,0:T(8,128)(2,1)S(1)}, bf16[64,2880]{1,0:T(8,128)(2,1)S(1)}, u32[]{:S(2)}, u32[]{:S(2)}) %collective-permute-start.10) | collective-permute-done | bytes 368672 | tf_op jit(solution)/shard_map/ppermute | solution.py:24
  77.5 1.6 collective-permute-done.11.refs_2_.refs_3_
  79.7 1.8 collective-permute-start.13
  82.3 1.5 collective-permute-start.15
  83.8 1.2 collective-permute-start.16
  85.0 1.0 shard_map.118
  86.1 9.1 %shard_map.119 = (bf16[64,2880]{1,0:T(8,128)(2,1)S(1)}, bf16[64,2880]{1,0:T(8,128)(2,1)S(1)}, bf16[64,2880]{1,0:T(8,128)(2,1)S(1)}, bf16[64,2880]{1,0:T(8,128)(2,1)S(1)}) custom-call(bf16[64,2880]{1,0:T(8,128)(2,1)S(1)} %get-tuple-element.93.refs_0_, bf16[64,2880]{1,0:T(8,128)(2,1)S(1)} %collective-permute-done.9.refs_0_.refs_1_, ...), custom_call_target="tpu_custom_call" | custom-call | flops 1 | bytes 1 | tf_op jit(solution)/shard_map/pallas_call | solution.py:346
  95.2 1.9 collective-permute-done.15.refs_1_.refs_2_
  97.6 1.3 collective-permute-start.17
  99.0 1.7 collective-permute-start.18
  100.7 0.9 collective-permute-start.19
  101.6 0.9 collective-permute-start.20
  102.5 1.0 shard_map.121
  103.5 9.1 %shard_map.122 = (bf16[64,2880]{1,0:T(8,128)(2,1)S(1)}, bf16[64,2880]{1,0:T(8,128)(2,1)S(1)}, bf16[64,2880]{1,0:T(8,128)(2,1)S(1)}, bf16[64,2880]{1,0:T(8,128)(2,1)S(1)}) custom-call(bf16[64,2880]{1,0:T(8,128)(2,1)S(1)} %get-tuple-element.103.refs_8_.refs_0_, bf16[64,2880]{1,0:T(8,128)(2,1)S(1)} %collective-permute-done.14.refs_0_.refs_1_, ...), custom_call_target="tpu_custom_call" | custom-call | flops 1 | bytes 1 | tf_op jit(solution)/shard_map/pallas_call | solution.py:346
  112.6 1.8 collective-permute-start.24
  114.3 0.9 collective-permute-start.25
  115.3 0.8 collective-permute-start.26
  117.1 1.3 collective-permute-start.21
  118.5 0.9 collective-permute-start.22
  119.4 9.1 %shard_map.124 = (bf16[64,2880]{1,0:T(8,128)(2,1)S(1)}, bf16[64,2880]{1,0:T(8,128)(2,1)S(1)}, bf16[64,2880]{1,0:T(8,128)(2,1)S(1)}, bf16[64,2880]{1,0:T(8,128)(2,1)S(1)}) custom-call(bf16[64,2880]{1,0:T(8,128)(2,1)S(1)} %get-tuple-element.123.refs_8_.refs_0_, bf16[64,2880]{1,0:T(8,128)(2,1)S(1)} %collective-permute-done.18.refs_0_.refs_1_, ...), custom_call_target="tpu_custom_call" | custom-call | flops 1 | bytes 1 | tf_op jit(solution)/shard_map/pallas_call | solution.py:346
  128.5 5.2 %collective-permute-done.25.refs_2_ = bf16[64,2880]{1,0:T(8,128)(2,1)S(1)} collective-permute-done((bf16[64,2880]{1,0:T(8,128)(2,1)S(1)}, bf16[64,2880]{1,0:T(8,128)(2,1)S(1)}, u32[]{:S(2)}, u32[]{:S(2)}) %collective-permute-start.25) | collective-permute-done | bytes 368672 | tf_op jit(solution)/shard_map/ppermute | solution.py:24
  134.9 1.6 collective-permute-start.33
  136.4 1.6 collective-permute-start.23
  138.0 2.9 %collective-permute-done.21.refs_1_ = bf16[64,2880]{1,0:T(8,128)(2,1)S(1)} collective-permute-done((bf16[64,2880]{1,0:T(8,128)(2,1)S(1)}, bf16[64,2880]{1,0:T(8,128)(2,1)S(1)}, u32[]{:S(2)}, u32[]{:S(2)}) %collective-permute-start.21) | collective-permute-done | bytes 368672 | tf_op jit(solution)/shard_map/ppermute | solution.py:24
  140.9 1.4 collective-permute-start.34
  142.3 1.3 collective-permute-start.35
  143.7 14.2 %collective-permute-done.23.refs_3_ = bf16[64,2880]{1,0:T(8,128)(2,1)S(1)} collective-permute-done((bf16[64,2880]{1,0:T(8,128)(2,1)S(1)}, bf16[64,2880]{1,0:T(8,128)(2,1)S(1)}, u32[]{:S(2)}, u32[]{:S(2)}) %collective-permute-start.23) | collective-permute-done | bytes 368672 | tf_op jit(solution)/shard_map/ppermute | solution.py:24
  157.8 7.7 %shard_map.126 = (bf16[64,2880]{1,0:T(8,128)(2,1)S(1)}, bf16[64,2880]{1,0:T(8,128)(2,1)S(1)}, bf16[64,2880]{1,0:T(8,128)(2,1)S(1)}, bf16[64,2880]{1,0:T(8,128)(2,1)S(1)}) custom-call(bf16[64,2880]{1,0:T(8,128)(2,1)S(1)} %get-tuple-element.130.refs_8_.refs_0_, bf16[64,2880]{1,0:T(8,128)(2,1)S(1)} %collective-permute-done.21.refs_1_, ...), custom_call_target="tpu_custom_call" | custom-call | flops 1 | bytes 1 | tf_op jit(solution)/shard_map/pallas_call | solution.py:346
  165.9 0.8 collective-permute-start.37
  166.8 1.1 collective-permute-start.30
  167.9 1.0 collective-permute-start.31
  168.9 1.4 collective-permute-start.32
  170.3 4.1 %collective-permute-done.30.refs_1_ = bf16[64,2880]{1,0:T(8,128)(2,1)S(1)} collective-permute-done((bf16[64,2880]{1,0:T(8,128)(2,1)S(1)}, bf16[64,2880]{1,0:T(8,128)(2,1)S(1)}, u32[]{:S(2)}, u32[]{:S(2)}) %collective-permute-start.30) | collective-permute-done | bytes 368672 | tf_op jit(solution)/shard_map/ppermute | solution.py:24
  174.4 2.8 %collective-permute-done.31.refs_2_ = bf16[64,2880]{1,0:T(8,128)(2,1)S(1)} collective-permute-done((bf16[64,2880]{1,0:T(8,128)(2,1)S(1)}, bf16[64,2880]{1,0:T(8,128)(2,1)S(1)}, u32[]{:S(2)}, u32[]{:S(2)}) %collective-permute-start.31) | collective-permute-done | bytes 368672 | tf_op jit(solution)/shard_map/ppermute | solution.py:24
  177.2 5.9 %collective-permute-done.32.refs_3_ = bf16[64,2880]{1,0:T(8,128)(2,1)S(1)} collective-permute-done((bf16[64,2880]{1,0:T(8,128)(2,1)S(1)}, bf16[64,2880]{1,0:T(8,128)(2,1)S(1)}, u32[]{:S(2)}, u32[]{:S(2)}) %collective-permute-start.32) | collective-permute-done | bytes 368672 | tf_op jit(solution)/shard_map/ppermute | solution.py:24
  183.6 1.0 collective-permute-start.28
  184.6 2.5 %collective-permute-start.29 = (bf16[64,2880]{1,0:T(8,128)(2,1)S(1)}, bf16[64,2880]{1,0:T(8,128)(2,1)S(1)}, u32[]{:S(2)}, u32[]{:S(2)}) collective-permute-start(bf16[64,2880]{1,0:T(8,128)(2,1)S(1)} %get-tuple-element.149), channel_id=1, source_target_pairs={{0,24},{8,16},{16,8},{24,0},{1,25},{9,17},{17,9},{25,1},{2,26},{10... | collective-permute-start | bytes 1105928 | tf_op jit(solution)/shard_map/ppermute | solution.py:24
  187.1 4.1 %collective-permute-done.27.refs_1_ = bf16[64,2880]{1,0:T(8,128)(2,1)S(1)} collective-permute-done((bf16[64,2880]{1,0:T(8,128)(2,1)S(1)}, bf16[64,2880]{1,0:T(8,128)(2,1)S(1)}, u32[]{:S(2)}, u32[]{:S(2)}) %collective-permute-start.27) | collective-permute-done | bytes 368672 | tf_op jit(solution)/shard_map/ppermute | solution.py:24
  191.2 4.5 %collective-permute-done.28.refs_2_ = bf16[64,2880]{1,0:T(8,128)(2,1)S(1)} collective-permute-done((bf16[64,2880]{1,0:T(8,128)(2,1)S(1)}, bf16[64,2880]{1,0:T(8,128)(2,1)S(1)}, u32[]{:S(2)}, u32[]{:S(2)}) %collective-permute-start.28) | collective-permute-done | bytes 368672 | tf_op jit(solution)/shard_map/ppermute | solution.py:24
  196.1 0.9 collective-permute-done.38.refs_1_
  197.1 1.1 copy.17
  (74 shorter events, 6.7 us)
Async XLA Ops:
  2.1 8.2 %collective-permute-start = (bf16[128,640]{1,0:T(8,128)(2,1)}, bf16[128,640]{1,0:T(8,128)(2,1)S(1)}, u32[]{:S(2)}, u32[]{:S(2)}) collective-permute-start(bf16[128,640]{1,0:T(8,128)(2,1)} %get-tuple-element.79), channel_id=1, source_target_pairs={{0,8},{8,0},{16,24},{24,16},{1,9},{9,1},{17,25},{25,17},{2,10},{10... | collective-permute-start | bytes 491528 | tf_op jit(solution)/shard_map/ppermute | solution.py:24
  5.1 9.4 %collective-permute-start.1 = (bf16[128,640]{1,0:T(8,128)(2,1)}, bf16[128,640]{1,0:T(8,128)(2,1)S(1)}, u32[]{:S(2)}, u32[]{:S(2)}) collective-permute-start(bf16[128,640]{1,0:T(8,128)(2,1)} %get-tuple-element.80), channel_id=1, source_target_pairs={{0,16},{8,24},{16,0},{24,8},{1,17},{9,25},{17,1},{25,9},{2,18},{10... | collective-permute-start | bytes 491528 | tf_op jit(solution)/shard_map/ppermute | solution.py:24
  6.6 7.9 %collective-permute-start.2 = (bf16[128,640]{1,0:T(8,128)(2,1)}, bf16[128,640]{1,0:T(8,128)(2,1)S(1)}, u32[]{:S(2)}, u32[]{:S(2)}) collective-permute-start(bf16[128,640]{1,0:T(8,128)(2,1)} %get-tuple-element.81), channel_id=1, source_target_pairs={{0,24},{8,16},{16,8},{24,0},{1,25},{9,17},{17,9},{25,1},{2,26},{10... | collective-permute-start | bytes 491528 | tf_op jit(solution)/shard_map/ppermute | solution.py:24
  10.3 4.7 %copy-start.2 = (bf16[128,640]{1,0:T(8,128)(2,1)}, bf16[128,640]{1,0:T(8,128)(2,1)S(1)}, u32[]{:S(2)}) copy-start(bf16[128,640]{1,0:T(8,128)(2,1)S(1)} %collective-permute-done.refs_1_) | copy-start | bytes 491524
  14.5 0.7 copy-start.3
  14.5 0.7 copy-start.4
  14.5 40.7 %collective-permute-start.7 = (bf16[1440,2880]{1,0:T(8,128)(2,1)}, bf16[1440,2880]{1,0:T(8,128)(2,1)}, u32[]{:S(2)}, u32[]{:S(2)}) collective-permute-start(bf16[1440,2880]{1,0:T(8,128)(2,1)} %bitcast.24), channel_id=1, source_target_pairs={{0,1},{1,0},{2,3},{3,2},{4,5},{5,4},{6,7},{7,6},{8,9},{9,8},{10,11... | collective-permute-start | bytes 24883208 | tf_op jit(solution)/shard_map/ppermute | solution.py:36
  14.6 36.6 %collective-permute-start.8 = (bf16[720,2880]{1,0:T(8,128)(2,1)}, bf16[720,2880]{1,0:T(8,128)(2,1)}, u32[]{:S(2)}, u32[]{:S(2)}) collective-permute-start(bf16[720,2880]{1,0:T(8,128)(2,1)} %bitcast.31), channel_id=1, source_target_pairs={{0,1},{1,0},{2,3},{3,2},{4,5},{5,4},{6,7},{7,6},{8,9},{9,8},{10,11... | collective-permute-start | bytes 12441608 | tf_op jit(solution)/shard_map/ppermute | solution.py:36
  15.2 15.6 %copy-start.7 = (f32[1,128,4]{1,2,0:T(4,128)S(1)}, f32[1,128,4]{1,2,0:T(4,128)}, u32[]{:S(2)}) copy-start(f32[1,128,4]{1,2,0:T(4,128)} %param.19) | copy-start | bytes 6148
  15.2 15.6 %copy-start.8 = (s32[1,128,4]{1,2,0:T(4,128)S(1)}, s32[1,128,4]{1,2,0:T(4,128)}, u32[]{:S(2)}) copy-start(s32[1,128,4]{1,2,0:T(4,128)} %param.18) | copy-start | bytes 6148
  15.2 27.8 %copy-start.6 = (f32[2880]{0:T(1024)S(1)}, f32[2880]{0:T(1024)}, u32[]{:S(2)}) copy-start(f32[2880]{0:T(1024)} %param.16) | copy-start | bytes 34564
  20.4 20.9 %collective-permute-start.3 = (bf16[2,64,2880]{2,1,0:T(8,128)(2,1)}, bf16[2,64,2880]{2,1,0:T(8,128)(2,1)S(1)}, u32[]{:S(2)}, u32[]{:S(2)}) collective-permute-start(bf16[2,64,2880]{2,1,0:T(8,128)(2,1)} %shard_map.110.refs_4_), channel_id=1, source_target_pairs={{0,24},{8,16},{16,8},{24,0},{1,25},{9,17},{17,9},{25,1},{2,26},{10... | collective-permute-start | bytes 2211848 | tf_op jit(solution)/shard_map/ppermute | solution.py:24
  28.7 30.4 %collective-permute-start.5 = (bf16[2,64,2880]{2,1,0:T(8,128)(2,1)}, bf16[2,64,2880]{2,1,0:T(8,128)(2,1)S(1)}, u32[]{:S(2)}, u32[]{:S(2)}) collective-permute-start(bf16[2,64,2880]{2,1,0:T(8,128)(2,1)} %get-tuple-element.89.refs_6_), channel_id=1, source_target_pairs={{0,16},{8,24},{16,0},{24,8},{1,17},{9,25},{17,1},{25,9},{2,18},{10... | collective-permute-start | bytes 2211848 | tf_op jit(solution)/shard_map/ppermute | solution.py:24
  30.0 29.2 %collective-permute-start.6 = (bf16[2,64,2880]{2,1,0:T(8,128)(2,1)}, bf16[2,64,2880]{2,1,0:T(8,128)(2,1)S(1)}, u32[]{:S(2)}, u32[]{:S(2)}) collective-permute-start(bf16[2,64,2880]{2,1,0:T(8,128)(2,1)} %get-tuple-element.90), channel_id=1, source_target_pairs={{0,8},{8,0},{16,24},{24,16},{1,9},{9,1},{17,25},{25,17},{2,10},{10... | collective-permute-start | bytes 2211848 | tf_op jit(solution)/shard_map/ppermute | solution.py:24
  41.4 1.7 copy-start.5
  41.4 8.5 %collective-permute-start.4 = (bf16[128,64]{1,0:T(8,128)(2,1)S(1)}, bf16[128,64]{1,0:T(8,128)(2,1)S(1)}, u32[]{:S(2)}, u32[]{:S(2)}) collective-permute-start(bf16[128,64]{1,0:T(8,128)(2,1)S(1)} %get-tuple-element.86), channel_id=1, source_target_pairs={{0,2},{1,3},{2,4},{3,5},{4,6},{5,7},{6,0},{7,1},{8,10},{9,11},{10,... | collective-permute-start | bytes 49160 | tf_op jit(solution)/shard_map/ppermute | solution.py:31
  51.1 1.4 copy-start
  52.5 2.7 %copy-start.1 = (f32[2,64,2880]{2,1,0:T(8,128)S(1)}, f32[2,64,2880]{2,1,0:T(8,128)}, u32[]{:S(2)}) copy-start(f32[2,64,2880]{2,1,0:T(8,128)} %shard_map.113.refs_0_) | copy-start | bytes 4423684
  59.2 26.8 %slice-start = ((s8[8478720]{0:T(1024)(128)(4,1)}), s8[4194304]{0:T(1024)(128)(4,1)S(1)}, s32[]{:S(2)}) async-start(s8[8478720]{0:T(1024)(128)(4,1)} %bitcast.25), calls=%async_computation | async-start | bytes 8388608
  59.2 26.8 %slice-start.3 = ((s8[4239360]{0:T(1024)(128)(4,1)}), s8[4194304]{0:T(1024)(128)(4,1)S(1)}, s32[]{:S(2)}) async-start(s8[4239360]{0:T(1024)(128)(4,1)} %bitcast.32), calls=%async_computation.3 | async-start | bytes 8388608
  59.2 26.8 %slice-start.1 = ((s8[8478720]{0:T(1024)(128)(4,1)}), s8[4194304]{0:T(1024)(128)(4,1)S(1)}, s32[]{:S(2)}) async-start(s8[8478720]{0:T(1024)(128)(4,1)} %bitcast.25), calls=%async_computation.1 | async-start | bytes 8388608
  59.2 26.8 %slice-start.2 = ((s8[8478720]{0:T(1024)(128)(4,1)}), s8[90112]{0:T(1024)(128)(4,1)S(1)}, s32[]{:S(2)}) async-start(s8[8478720]{0:T(1024)(128)(4,1)} %bitcast.25), calls=%async_computation.2 | async-start | bytes 180224
  59.2 26.8 %slice-start.4 = ((s8[4239360]{0:T(1024)(128)(4,1)}), s8[45056]{0:T(1024)(128)(4,1)S(1)}, s32[]{:S(2)}) async-start(s8[4239360]{0:T(1024)(128)(4,1)} %bitcast.32), calls=%async_computation.4 | async-start | bytes 90112
  60.2 18.9 %collective-permute-start.12 = (bf16[2,64,2944]{2,1,0:T(8,128)(2,1)S(1)}, bf16[2,64,2944]{2,1,0:T(8,128)(2,1)S(1)}, u32[]{:S(2)}, u32[]{:S(2)}) collective-permute-start(bf16[2,64,2944]{2,1,0:T(8,128)(2,1)S(1)} %get-tuple-element.97), channel_id=1, source_target_pairs={{0,2},{1,3},{2,4},{3,5},{4,6},{5,7},{6,0},{7,1},{8,10},{9,11},{10,... | collective-permute-start | bytes 2261000 | tf_op jit(solution)/shard_map/ppermute | solution.py:31
  61.9 11.7 %collective-permute-start.9 = (bf16[64,2880]{1,0:T(8,128)(2,1)S(1)}, bf16[64,2880]{1,0:T(8,128)(2,1)S(1)}, u32[]{:S(2)}, u32[]{:S(2)}) collective-permute-start(bf16[64,2880]{1,0:T(8,128)(2,1)S(1)} %get-tuple-element.94), channel_id=1, source_target_pairs={{0,8},{8,0},{16,24},{24,16},{1,9},{9,1},{17,25},{25,17},{2,10},{10... | collective-permute-start | bytes 1105928 | tf_op jit(solution)/shard_map/ppermute | solution.py:24
  63.0 14.4 %collective-permute-start.10 = (bf16[64,2880]{1,0:T(8,128)(2,1)S(1)}, bf16[64,2880]{1,0:T(8,128)(2,1)S(1)}, u32[]{:S(2)}, u32[]{:S(2)}) collective-permute-start(bf16[64,2880]{1,0:T(8,128)(2,1)S(1)} %get-tuple-element.95), channel_id=1, source_target_pairs={{0,16},{8,24},{16,0},{24,8},{1,17},{9,25},{17,1},{25,9},{2,18},{10... | collective-permute-start | bytes 1105928 | tf_op jit(solution)/shard_map/ppermute | solution.py:24
  63.9 15.2 %collective-permute-start.11 = (bf16[64,2880]{1,0:T(8,128)(2,1)S(1)}, bf16[64,2880]{1,0:T(8,128)(2,1)S(1)}, u32[]{:S(2)}, u32[]{:S(2)}) collective-permute-start(bf16[64,2880]{1,0:T(8,128)(2,1)S(1)} %get-tuple-element.96), channel_id=1, source_target_pairs={{0,24},{8,16},{16,8},{24,0},{1,25},{9,17},{17,9},{25,1},{2,26},{10... | collective-permute-start | bytes 1105928 | tf_op jit(solution)/shard_map/ppermute | solution.py:24
  79.7 17.4 %collective-permute-start.13 = (bf16[2,64,2944]{2,1,0:T(8,128)(2,1)S(1)}, bf16[2,64,2944]{2,1,0:T(8,128)(2,1)S(1)}, u32[]{:S(2)}, u32[]{:S(2)}) collective-permute-start(bf16[2,64,2944]{2,1,0:T(8,128)(2,1)S(1)} %collective-permute-done.12.held_ref.refs_0_), channel_id=1, source_target_pairs={{0,2},{1,3},{2,4},{3,5},{4,6},{5,7},{6,0},{7,1},{8,10},{9,11},{10,... | collective-permute-start | bytes 2261000 | tf_op jit(solution)/shard_map/ppermute | solution.py:31
  81.5 13.7 %collective-permute-start.14 = (bf16[64,2880]{1,0:T(8,128)(2,1)S(1)}, bf16[64,2880]{1,0:T(8,128)(2,1)S(1)}, u32[]{:S(2)}, u32[]{:S(2)}) collective-permute-start(bf16[64,2880]{1,0:T(8,128)(2,1)S(1)} %get-tuple-element.111), channel_id=1, source_target_pairs={{0,8},{8,0},{16,24},{24,16},{1,9},{9,1},{17,25},{25,17},{2,10},{10... | collective-permute-start | bytes 1105928 | tf_op jit(solution)/shard_map/ppermute | solution.py:24
  82.3 14.7 %collective-permute-start.15 = (bf16[64,2880]{1,0:T(8,128)(2,1)S(1)}, bf16[64,2880]{1,0:T(8,128)(2,1)S(1)}, u32[]{:S(2)}, u32[]{:S(2)}) collective-permute-start(bf16[64,2880]{1,0:T(8,128)(2,1)S(1)} %get-tuple-element.112), channel_id=1, source_target_pairs={{0,16},{8,24},{16,0},{24,8},{1,17},{9,25},{17,1},{25,9},{2,18},{10... | collective-permute-start | bytes 1105928 | tf_op jit(solution)/shard_map/ppermute | solution.py:24
  83.8 13.2 %collective-permute-start.16 = (bf16[64,2880]{1,0:T(8,128)(2,1)S(1)}, bf16[64,2880]{1,0:T(8,128)(2,1)S(1)}, u32[]{:S(2)}, u32[]{:S(2)}) collective-permute-start(bf16[64,2880]{1,0:T(8,128)(2,1)S(1)} %get-tuple-element.113), channel_id=1, source_target_pairs={{0,24},{8,16},{16,8},{24,0},{1,25},{9,17},{17,9},{25,1},{2,26},{10... | collective-permute-start | bytes 1105928 | tf_op jit(solution)/shard_map/ppermute | solution.py:24
  97.6 19.0 %collective-permute-start.17 = (bf16[2,64,2944]{2,1,0:T(8,128)(2,1)S(1)}, bf16[2,64,2944]{2,1,0:T(8,128)(2,1)S(1)}, u32[]{:S(2)}, u32[]{:S(2)}) collective-permute-start(bf16[2,64,2944]{2,1,0:T(8,128)(2,1)S(1)} %collective-permute-done.13.held_ref.refs_0_), channel_id=1, source_target_pairs={{0,2},{1,3},{2,4},{3,5},{4,6},{5,7},{6,0},{7,1},{8,10},{9,11},{10,... | collective-permute-start | bytes 2261000 | tf_op jit(solution)/shard_map/ppermute | solution.py:31
  99.0 15.4 %collective-permute-start.18 = (bf16[64,2880]{1,0:T(8,128)(2,1)S(1)}, bf16[64,2880]{1,0:T(8,128)(2,1)S(1)}, u32[]{:S(2)}, u32[]{:S(2)}) collective-permute-start(bf16[64,2880]{1,0:T(8,128)(2,1)S(1)} %get-tuple-element.120), channel_id=1, source_target_pairs={{0,8},{8,0},{16,24},{24,16},{1,9},{9,1},{17,25},{25,17},{2,10},{10... | collective-permute-start | bytes 1105928 | tf_op jit(solution)/shard_map/ppermute | solution.py:24
  100.7 14.6 %collective-permute-start.19 = (bf16[64,2880]{1,0:T(8,128)(2,1)S(1)}, bf16[64,2880]{1,0:T(8,128)(2,1)S(1)}, u32[]{:S(2)}, u32[]{:S(2)}) collective-permute-start(bf16[64,2880]{1,0:T(8,128)(2,1)S(1)} %get-tuple-element.121), channel_id=1, source_target_pairs={{0,16},{8,24},{16,0},{24,8},{1,17},{9,25},{17,1},{25,9},{2,18},{10... | collective-permute-start | bytes 1105928 | tf_op jit(solution)/shard_map/ppermute | solution.py:24
  101.6 15.0 %collective-permute-start.20 = (bf16[64,2880]{1,0:T(8,128)(2,1)S(1)}, bf16[64,2880]{1,0:T(8,128)(2,1)S(1)}, u32[]{:S(2)}, u32[]{:S(2)}) collective-permute-start(bf16[64,2880]{1,0:T(8,128)(2,1)S(1)} %get-tuple-element.122), channel_id=1, source_target_pairs={{0,24},{8,16},{16,8},{24,0},{1,25},{9,17},{17,9},{25,1},{2,26},{10... | collective-permute-start | bytes 1105928 | tf_op jit(solution)/shard_map/ppermute | solution.py:24
  112.6 15.9 %collective-permute-start.24 = (bf16[64,2880]{1,0:T(8,128)(2,1)S(1)}, bf16[64,2880]{1,0:T(8,128)(2,1)S(1)}, u32[]{:S(2)}, u32[]{:S(2)}) collective-permute-start(bf16[64,2880]{1,0:T(8,128)(2,1)S(1)} %get-tuple-element.135), channel_id=1, source_target_pairs={{0,8},{8,0},{16,24},{24,16},{1,9},{9,1},{17,25},{25,17},{2,10},{10... | collective-permute-start | bytes 1105928 | tf_op jit(solution)/shard_map/ppermute | solution.py:24
  114.3 19.4 %collective-permute-start.25 = (bf16[64,2880]{1,0:T(8,128)(2,1)S(1)}, bf16[64,2880]{1,0:T(8,128)(2,1)S(1)}, u32[]{:S(2)}, u32[]{:S(2)}) collective-permute-start(bf16[64,2880]{1,0:T(8,128)(2,1)S(1)} %get-tuple-element.136), channel_id=1, source_target_pairs={{0,16},{8,24},{16,0},{24,8},{1,17},{9,25},{17,1},{25,9},{2,18},{10... | collective-permute-start | bytes 1105928 | tf_op jit(solution)/shard_map/ppermute | solution.py:24
  115.3 18.4 %collective-permute-start.26 = (bf16[64,2880]{1,0:T(8,128)(2,1)S(1)}, bf16[64,2880]{1,0:T(8,128)(2,1)S(1)}, u32[]{:S(2)}, u32[]{:S(2)}) collective-permute-start(bf16[64,2880]{1,0:T(8,128)(2,1)S(1)} %get-tuple-element.137), channel_id=1, source_target_pairs={{0,24},{8,16},{16,8},{24,0},{1,25},{9,17},{17,9},{25,1},{2,26},{10... | collective-permute-start | bytes 1105928 | tf_op jit(solution)/shard_map/ppermute | solution.py:24
  117.1 23.8 %collective-permute-start.21 = (bf16[64,2880]{1,0:T(8,128)(2,1)S(1)}, bf16[64,2880]{1,0:T(8,128)(2,1)S(1)}, u32[]{:S(2)}, u32[]{:S(2)}) collective-permute-start(bf16[64,2880]{1,0:T(8,128)(2,1)S(1)} %get-tuple-element.131), channel_id=1, source_target_pairs={{0,8},{8,0},{16,24},{24,16},{1,9},{9,1},{17,25},{25,17},{2,10},{10... | collective-permute-start | bytes 1105928 | tf_op jit(solution)/shard_map/ppermute | solution.py:24
  118.5 23.9 %collective-permute-start.22 = (bf16[64,2880]{1,0:T(8,128)(2,1)S(1)}, bf16[64,2880]{1,0:T(8,128)(2,1)S(1)}, u32[]{:S(2)}, u32[]{:S(2)}) collective-permute-start(bf16[64,2880]{1,0:T(8,128)(2,1)S(1)} %get-tuple-element.132), channel_id=1, source_target_pairs={{0,16},{8,24},{16,0},{24,8},{1,17},{9,25},{17,1},{25,9},{2,18},{10... | collective-permute-start | bytes 1105928 | tf_op jit(solution)/shard_map/ppermute | solution.py:24
  134.1 31.4 %collective-permute-start.36 = (bf16[2,64,2880]{2,1,0:T(8,128)(2,1)S(1)}, bf16[2,64,2880]{2,1,0:T(8,128)(2,1)S(1)}, u32[]{:S(2)}, u32[]{:S(2)}) collective-permute-start(bf16[2,64,2880]{2,1,0:T(8,128)(2,1)S(1)} %shard_map.125.refs_8_), channel_id=1, source_target_pairs={{0,2},{1,3},{2,4},{3,5},{4,6},{5,7},{6,0},{7,1},{8,10},{9,11},{10,... | collective-permute-start | bytes 2211848 | tf_op jit(solution)/shard_map/ppermute | solution.py:31
  134.9 30.6 %collective-permute-start.33 = (bf16[64,2880]{1,0:T(8,128)(2,1)S(1)}, bf16[64,2880]{1,0:T(8,128)(2,1)S(1)}, u32[]{:S(2)}, u32[]{:S(2)}) collective-permute-start(bf16[64,2880]{1,0:T(8,128)(2,1)S(1)} %get-tuple-element.139.refs_5_), channel_id=1, source_target_pairs={{0,8},{8,0},{16,24},{24,16},{1,9},{9,1},{17,25},{25,17},{2,10},{10... | collective-permute-start | bytes 1105928 | tf_op jit(solution)/shard_map/ppermute | solution.py:24
  136.4 21.4 %collective-permute-start.23 = (bf16[64,2880]{1,0:T(8,128)(2,1)S(1)}, bf16[64,2880]{1,0:T(8,128)(2,1)S(1)}, u32[]{:S(2)}, u32[]{:S(2)}) collective-permute-start(bf16[64,2880]{1,0:T(8,128)(2,1)S(1)} %get-tuple-element.133), channel_id=1, source_target_pairs={{0,24},{8,16},{16,8},{24,0},{1,25},{9,17},{17,9},{25,1},{2,26},{10... | collective-permute-start | bytes 1105928 | tf_op jit(solution)/shard_map/ppermute | solution.py:24
  140.9 24.6 %collective-permute-start.34 = (bf16[64,2880]{1,0:T(8,128)(2,1)S(1)}, bf16[64,2880]{1,0:T(8,128)(2,1)S(1)}, u32[]{:S(2)}, u32[]{:S(2)}) collective-permute-start(bf16[64,2880]{1,0:T(8,128)(2,1)S(1)} %get-tuple-element.140.refs_6_), channel_id=1, source_target_pairs={{0,16},{8,24},{16,0},{24,8},{1,17},{9,25},{17,1},{25,9},{2,18},{10... | collective-permute-start | bytes 1105928 | tf_op jit(solution)/shard_map/ppermute | solution.py:24
  142.3 23.2 %collective-permute-start.35 = (bf16[64,2880]{1,0:T(8,128)(2,1)S(1)}, bf16[64,2880]{1,0:T(8,128)(2,1)S(1)}, u32[]{:S(2)}, u32[]{:S(2)}) collective-permute-start(bf16[64,2880]{1,0:T(8,128)(2,1)S(1)} %get-tuple-element.141.refs_7_), channel_id=1, source_target_pairs={{0,24},{8,16},{16,8},{24,0},{1,25},{9,17},{17,9},{25,1},{2,26},{10... | collective-permute-start | bytes 1105928 | tf_op jit(solution)/shard_map/ppermute | solution.py:24
  165.9 17.2 %collective-permute-start.37 = (bf16[2,64,2880]{2,1,0:T(8,128)(2,1)S(1)}, bf16[2,64,2880]{2,1,0:T(8,128)(2,1)S(1)}, u32[]{:S(2)}, u32[]{:S(2)}) collective-permute-start(bf16[2,64,2880]{2,1,0:T(8,128)(2,1)S(1)} %shard_map.127.refs_5_), channel_id=1, source_target_pairs={{0,2},{1,3},{2,4},{3,5},{4,6},{5,7},{6,0},{7,1},{8,10},{9,11},{10,... | collective-permute-start | bytes 2211848 | tf_op jit(solution)/shard_map/ppermute | solution.py:31
  166.8 7.6 %collective-permute-start.30 = (bf16[64,2880]{1,0:T(8,128)(2,1)S(1)}, bf16[64,2880]{1,0:T(8,128)(2,1)S(1)}, u32[]{:S(2)}, u32[]{:S(2)}) collective-permute-start(bf16[64,2880]{1,0:T(8,128)(2,1)S(1)} %get-tuple-element.143.refs_6_), channel_id=1, source_target_pairs={{0,8},{8,0},{16,24},{24,16},{1,9},{9,1},{17,25},{25,17},{2,10},{10... | collective-permute-start | bytes 1105928 | tf_op jit(solution)/shard_map/ppermute | solution.py:24
  167.9 9.3 %collective-permute-start.31 = (bf16[64,2880]{1,0:T(8,128)(2,1)S(1)}, bf16[64,2880]{1,0:T(8,128)(2,1)S(1)}, u32[]{:S(2)}, u32[]{:S(2)}) collective-permute-start(bf16[64,2880]{1,0:T(8,128)(2,1)S(1)} %get-tuple-element.144.refs_7_), channel_id=1, source_target_pairs={{0,16},{8,24},{16,0},{24,8},{1,17},{9,25},{17,1},{25,9},{2,18},{10... | collective-permute-start | bytes 1105928 | tf_op jit(solution)/shard_map/ppermute | solution.py:24
  168.9 14.2 %collective-permute-start.32 = (bf16[64,2880]{1,0:T(8,128)(2,1)S(1)}, bf16[64,2880]{1,0:T(8,128)(2,1)S(1)}, u32[]{:S(2)}, u32[]{:S(2)}) collective-permute-start(bf16[64,2880]{1,0:T(8,128)(2,1)S(1)} %get-tuple-element.145.refs_8_), channel_id=1, source_target_pairs={{0,24},{8,16},{16,8},{24,0},{1,25},{9,17},{17,9},{25,1},{2,26},{10... | collective-permute-start | bytes 1105928 | tf_op jit(solution)/shard_map/ppermute | solution.py:24
  183.5 13.5 %collective-permute-start.38 = (bf16[2,64,2880]{2,1,0:T(8,128)(2,1)S(1)}, bf16[2,64,2880]{2,1,0:T(8,128)(2,1)S(1)}, u32[]{:S(2)}, u32[]{:S(2)}) collective-permute-start(bf16[2,64,2880]{2,1,0:T(8,128)(2,1)S(1)} %shard_map.128.refs_5_), channel_id=1, source_target_pairs={{0,2},{1,3},{2,4},{3,5},{4,6},{5,7},{6,0},{7,1},{8,10},{9,11},{10,... | collective-permute-start | bytes 2211848 | tf_op jit(solution)/shard_map/ppermute | solution.py:31
  183.6 7.7 %collective-permute-start.27 = (bf16[64,2880]{1,0:T(8,128)(2,1)S(1)}, bf16[64,2880]{1,0:T(8,128)(2,1)S(1)}, u32[]{:S(2)}, u32[]{:S(2)}) collective-permute-start(bf16[64,2880]{1,0:T(8,128)(2,1)S(1)} %get-tuple-element.147), channel_id=1, source_target_pairs={{0,8},{8,0},{16,24},{24,16},{1,9},{9,1},{17,25},{25,17},{2,10},{10... | collective-permute-start | bytes 1105928 | tf_op jit(solution)/shard_map/ppermute | solution.py:24
  183.6 12.1 %collective-permute-start.28 = (bf16[64,2880]{1,0:T(8,128)(2,1)S(1)}, bf16[64,2880]{1,0:T(8,128)(2,1)S(1)}, u32[]{:S(2)}, u32[]{:S(2)}) collective-permute-start(bf16[64,2880]{1,0:T(8,128)(2,1)S(1)} %get-tuple-element.148), channel_id=1, source_target_pairs={{0,16},{8,24},{16,0},{24,8},{1,17},{9,25},{17,1},{25,9},{2,18},{10... | collective-permute-start | bytes 1105928 | tf_op jit(solution)/shard_map/ppermute | solution.py:24
  184.6 11.1 %collective-permute-start.29 = (bf16[64,2880]{1,0:T(8,128)(2,1)S(1)}, bf16[64,2880]{1,0:T(8,128)(2,1)S(1)}, u32[]{:S(2)}, u32[]{:S(2)}) collective-permute-start(bf16[64,2880]{1,0:T(8,128)(2,1)S(1)} %get-tuple-element.149), channel_id=1, source_target_pairs={{0,24},{8,16},{16,8},{24,0},{1,25},{9,17},{17,9},{25,1},{2,26},{10... | collective-permute-start | bytes 1105928 | tf_op jit(solution)/shard_map/ppermute | solution.py:24
